TPU v7x, 32 devices: a whole 2x2x4 slice. The times are simulated.
32 devices in a mesh: shell: 1, row: 4 (over z), col: 8 (over y, x, core).
Axes of the slice: x: 2, y: 2, z: 4, core: 2. Of those that a mesh axis runs over, the one named last changes fastest.
Arguments:
- convergence: bfloat16 [1, 16384, 16384], P('shell', ('row', 'col')), may hold values from -6 to 6
- lens_weight: float32 [1], P('shell'), may hold values from 0.3 to 1
- rays_in: float32 [6, 1024, 16384], P(None, ('row', 'col')), may hold values from -6 to 6
Outputs:
- rays_out: float32 [1, 6, 1024, 16384], P('shell', None, ('row', 'col'))
All inputs are finite; a program needn't handle non-finite values.
Results may differ from a plain program's by a relative error of at most 0.0003.
Values sent between devices are 32-bit elements; how exact they have to be, the bound alone decides.
No kernel may reach another device: no remote copies, remote signals or barrier semaphores. Data moves between devices by JAX's collectives and lax.ppermute only.
A program may use at most 256 MiB of HBM per device.

v0:
```python
import math

import jax
import jax.numpy as jnp
from jax import lax
from jax.sharding import PartitionSpec as P

STRIDE = 16


HIGHEST = lax.Precision.HIGHEST
SPLIT_THREE = lax.Precision.HIGH


def passed_along(value, axis, steps):
    count = lax.axis_size(axis)
    leading, last = (max(0, -steps), min(count, count - steps))
    return lax.ppermute(value, axis, [(source, source + steps) for source in range(leading, last)])


def product(form, left, right):
    return jnp.einsum(form, left, right, precision=HIGHEST, preferred_element_type=jnp.float32)


def product_input(form, left, right):
    return jnp.einsum(form, left, right, precision=SPLIT_THREE, preferred_element_type=jnp.float32)


def counting(length):
    return jnp.arange(length, dtype=jnp.int32)


def phases(first, second, length, sign):
    whole = first[:, None] * second[None, :] % length
    angle = sign * 2.0 * math.pi / length * whole.astype(jnp.float32)
    return (jnp.cos(angle), jnp.sin(angle))


def complex_section(form, real, imaginary, table):
    cosine, sine = table
    return (
        product(form, real, cosine) - product(form, imaginary, sine),
        product(form, real, sine) + product(form, imaginary, cosine),
    )


def twiddle(real, imaginary, table):
    cosine, sine = table
    return (real * cosine - imaginary * sine, real * sine + imaginary * cosine)


def column_spectrum(field, devices):
    rows_dev, length = field.shape
    block = length // (2 * devices)
    shaped = field.reshape(rows_dev, block, 2 * devices)
    cosine, sine = phases(counting(block), counting(block), block, -1.0)
    real = product_input("rvu,vt->rtu", shaped, cosine)
    imaginary = product_input("rvu,vt->rtu", shaped, sine)
    real, imaginary = twiddle(
        real, imaginary, phases(counting(block), counting(2 * devices), length, -1.0)
    )
    real, imaginary = complex_section(
        "rtu,ub->btr",
        real,
        imaginary,
        phases(counting(2 * devices), counting(devices), 2 * devices, -1.0),
    )
    return jnp.stack([real, imaginary]).reshape(2, devices * block, rows_dev)


def row_spectrum(arrived, order, rows_dev):
    block, length = (arrived.shape[1], arrived.shape[2])
    devices = length // rows_dev
    real = arrived[0].reshape(block, devices, rows_dev)
    imaginary = arrived[1].reshape(block, devices, rows_dev)
    real, imaginary = complex_section(
        "tpn,pk->tkn", real, imaginary, phases(order, counting(devices), devices, -1.0)
    )
    real, imaginary = twiddle(
        real, imaginary, phases(counting(devices), counting(rows_dev), length, -1.0)
    )
    real, imaginary = complex_section(
        "tkn,nj->tjk",
        real,
        imaginary,
        phases(counting(rows_dev), counting(rows_dev), rows_dev, -1.0),
    )
    return (real.reshape(block, length), imaginary.reshape(block, length))


def potential(real, imaginary, first_bin):
    block, length = real.shape
    half = length // 2
    frequency = counting(length)
    signed = jnp.where(frequency < half, frequency, frequency - length).astype(jnp.float32)
    wave_rows = (2.0 * math.pi / length * signed)[None, :]
    wave_cols = (2.0 * math.pi / length * (first_bin + counting(block)).astype(jnp.float32))[
        :, None
    ]
    squared = wave_rows * wave_rows + wave_cols * wave_cols
    valid = (squared > 0.0) & (frequency != half)[None, :]
    scale = jnp.where(valid, -2.0 / jnp.where(valid, squared, 1.0), 0.0) / (
        float(length) * float(length)
    )
    return (real * scale, imaginary * scale, wave_rows, wave_cols)


def ray_rows(real, imaginary, rays_dev):
    fields, block, length = real.shape
    rays = length // STRIDE
    devices = rays // rays_dev
    real = (
        real.reshape(fields, block, STRIDE, rays)
        .sum(axis=2)
        .reshape(fields, block, rays_dev, devices)
    )
    imaginary = (
        imaginary.reshape(fields, block, STRIDE, rays)
        .sum(axis=2)
        .reshape(fields, block, rays_dev, devices)
    )
    real, imaginary = complex_section(
        "ftqp,qa->ftap",
        real,
        imaginary,
        phases(counting(rays_dev), counting(rays_dev), rays_dev, 1.0),
    )
    real, imaginary = twiddle(
        real, imaginary, phases(counting(rays_dev), counting(devices), rays, 1.0)
    )
    real, imaginary = complex_section(
        "ftap,pz->fzat", real, imaginary, phases(counting(devices), counting(devices), devices, 1.0)
    )
    joined = jnp.stack(
        [real.reshape(fields, rays, block), imaginary.reshape(fields, rays, block)], axis=2
    )
    return joined.reshape(fields, rays, 2 * block)


def column_fields(real, imaginary, order, length):
    devices, block = (real.shape[2], real.shape[3])
    bins = order[:, None] * block + counting(block)[None, :]
    weight = jnp.where(bins == 0, 1.0, 2.0).astype(jnp.float32)
    real, imaginary = complex_section(
        "fypt,pu->fytu",
        real * weight,
        imaginary * weight,
        phases(order, counting(2 * devices), 2 * devices, 1.0),
    )
    real, imaginary = twiddle(
        real, imaginary, phases(counting(block), counting(2 * devices), length, 1.0)
    )
    cosine, sine = phases(counting(block), counting(block), block, 1.0)
    result = product("fytu,tv->fyvu", real, cosine) - product("fytu,tv->fyvu", imaginary, sine)
    return result.reshape(result.shape[0], result.shape[1], length)


def advance(state, fields, weight):
    shift_rows = state[0] - weight * fields[0]
    shift_cols = state[1] - weight * fields[1]
    curve_rows, curve_cols, curve_mixed = (fields[2], fields[3], fields[4])
    upper_left, upper_right, lower_left, lower_right = (state[2], state[3], state[4], state[5])
    new_ul = upper_left - weight * (curve_rows * upper_left + curve_mixed * lower_left)
    new_ur = upper_right - weight * (curve_rows * upper_right + curve_mixed * lower_right)
    new_ll = lower_left - weight * (curve_mixed * upper_left + curve_cols * lower_left)
    new_lr = lower_right - weight * (curve_mixed * upper_right + curve_cols * lower_right)
    return jnp.stack([shift_rows, shift_cols, new_ul, new_ur, new_ll, new_lr])


def body(convergence, lens_weight, rays_in):
    rows_axis = lax.axis_size("row")
    cols_axis = lax.axis_size("col")
    devices = rows_axis * cols_axis
    shells_dev, rows_dev, length = convergence.shape
    block = length // (2 * devices)
    first_bin = (lax.axis_index("row") * cols_axis + lax.axis_index("col")) * block
    position = counting(devices)
    all_fields = []
    spectrum = column_spectrum(convergence[0], devices)
    arrived = lax.all_to_all(spectrum, ("row", "col"), split_axis=1, concat_axis=2, tiled=True)
    real, imaginary = row_spectrum(arrived, position, rows_dev)
    real, imaginary, wave_rows, wave_cols = potential(real, imaginary, first_bin)
    stacked_real = jnp.stack([real, wave_rows * real, wave_rows * wave_rows * real])
    stacked_imaginary = jnp.stack(
        [imaginary, wave_rows * imaginary, wave_rows * wave_rows * imaginary]
    )
    outgoing = ray_rows(stacked_real, stacked_imaginary, rows_dev // STRIDE)
    returned = lax.all_to_all(outgoing, ("row", "col"), split_axis=1, concat_axis=2, tiled=True)
    returned = returned.reshape(returned.shape[0], returned.shape[1], devices, 2, block)
    back_real = returned[:, :, :, 0, :]
    back_imaginary = returned[:, :, :, 1, :]
    bins = (position[:, None] * block + counting(block)[None, :]).astype(jnp.float32)
    wave_bins = 2.0 * math.pi / length * bins
    back_real = jnp.stack(
        [
            -back_imaginary[1],
            -wave_bins * back_imaginary[0],
            -back_real[2],
            -wave_bins * wave_bins * back_real[0],
            -wave_bins * back_real[1],
        ]
    )
    back_imaginary = jnp.stack(
        [
            returned[1, :, :, 0, :],
            wave_bins * returned[0, :, :, 0, :],
            -returned[2, :, :, 1, :],
            -wave_bins * wave_bins * returned[0, :, :, 1, :],
            -wave_bins * returned[1, :, :, 1, :],
        ]
    )
    all_fields.append(column_fields(back_real, back_imaginary, position, length))

    def run_local(start):
        current = start
        current = advance(current, all_fields[0], lens_weight[0])
        results = [current]
        return jnp.stack(results)

    shell_index = lax.axis_index("shell")
    outputs = run_local(rays_in)
    for group in range(1, lax.axis_size("shell")):
        received = passed_along(outputs[-1], "shell", 1)
        outputs = jnp.where(shell_index == group, run_local(received), outputs)
    return outputs


def solution(mesh):
    in_specs = (P("shell", ("row", "col"), None), P("shell"), P(None, ("row", "col"), None))
    out_specs = P("shell", None, ("row", "col"), None)
    return jax.shard_map(body, mesh=mesh, in_specs=in_specs, out_specs=out_specs, check_vma=False)
```

profile of v0, /device:TPU:0, one launch (start us, length us, event | category | flops | bytes accessed | tf_op | source)
XLA Modules:
  0.0 2209.6 jit_solution(8500905182318804953)
XLA Ops:
  0.3 22.5 %copy.107 = bf16[1,512,16384]{1,2,0:T(8,128)(2,1)} copy(bf16[1,512,16384]{2,1,0:T(8,128)(2,1)} %param.3) | data formatting | bytes 33554432 | tf_op args[0]
  22.7 24.1 %copy.109 = bf16[512,256,64]{1,0,2:T(8,128)(2,1)} copy(bf16[512,256,64]{0,2,1:T(8,128)(2,1)} %bitcast.207) | data formatting | bytes 33554432 | tf_op jit(solution)/shard_map/reshape;squeeze | solution.py:55
  46.8 31.4 %fusion.104 = f32[256,512,64]{1,0,2:T(8,128)} fusion(bf16[512,256,64]{1,0,2:T(8,128)(2,1)} %copy.109), kind=kOutput, calls=%fused_computation.135 | convolution fusion | flops 12885819392 | bytes 50331648 | tf_op jit(solution)/shard_map/rvu,vt->rtu/dot_general | solution.py:26
  78.3 50.6 %add_bitcast_fusion = (f32[512,256,64]{0,1,2:T(8,128)}, f32[512,256,64]{0,1,2:T(8,128)}) fusion(f32[256,512,64]{1,0,2:T(8,128)} %fusion.104, f32[256,64]{0,1:T(8,128)S(1)} %get-tuple-element.47, f32[256,64]{0,1:T(8,128)S(1)} %get-tuple-element.48, bf16[512,256,64]{1,0,2:T(8,128)(2,1)} %copy.109), kind=kOutput, calls=%fused_computation.4 | convolution fusion | flops 12936151040 | bytes 117571584 | tf_op jit(solution)/shard_map/rvu,vt->rtu/dot_general | solution.py:26
  128.8 34.5 %copy.112 = f32[512,256,64]{1,2,0:T(8,128)} copy(f32[512,256,64]{0,1,2:T(8,128)} %get-tuple-element.10) | data formatting | bytes 67108864 | tf_op jit(solution)/shard_map/sub | solution.py:49
  163.3 23.9 %fusion.167 = f32[32,512,256]{2,0,1:T(8,128)} fusion(f32[512,256,64]{1,2,0:T(8,128)} %copy.112), kind=kOutput, calls=%fused_computation.219 | convolution fusion | flops 3221254144 | bytes 50331648 | tf_op jit(solution)/shard_map/rtu,ub->btr/dot_general | solution.py:22
  187.2 23.9 %fusion.171 = f32[32,512,256]{2,0,1:T(8,128)} fusion(f32[512,256,64]{1,2,0:T(8,128)} %copy.112), kind=kOutput, calls=%fused_computation.223 | convolution fusion | flops 3221254144 | bytes 50331648 | tf_op jit(solution)/shard_map/rtu,ub->btr/dot_general | solution.py:22
  211.1 34.5 %copy.113 = f32[512,256,64]{1,2,0:T(8,128)} copy(f32[512,256,64]{0,1,2:T(8,128)} %get-tuple-element.9) | data formatting | bytes 67108864 | tf_op jit(solution)/shard_map/add | solution.py:49
  245.6 27.9 %subtract_bitcast_fusion.3 = f32[32,256,512]{1,0,2:T(8,128)} fusion(f32[32,512,256]{2,0,1:T(8,128)} %fusion.171, f32[512,256,64]{1,2,0:T(8,128)} %copy.113), kind=kOutput, calls=%fused_computation.18 | convolution fusion | flops 3225448448 | bytes 67108864 | tf_op jit(solution)/shard_map/rtu,ub->btr/dot_general | solution.py:22
  273.5 27.6 %add_bitcast_fusion.3 = f32[32,256,512]{1,0,2:T(8,128)} fusion(f32[32,512,256]{2,0,1:T(8,128)} %fusion.167, f32[512,256,64]{1,2,0:T(8,128)} %copy.113), kind=kOutput, calls=%fused_computation.17 | convolution fusion | flops 3225448448 | bytes 67108864 | tf_op jit(solution)/shard_map/rtu,ub->btr/dot_general | solution.py:22
  301.1 18.2 stack.21
  319.3 35.0 %copy.117 = f32[1,8192,512]{2,0,1:T(1,128)} copy(f32[1,8192,512]{1,2,0:T(8,128)} %stack.21) | data formatting | bytes 33554432 | tf_op jit(solution)/shard_map/stack | solution.py:68
  354.3 18.2 stack.20
  372.6 34.9 %copy.116 = f32[1,8192,512]{2,0,1:T(1,128)} copy(f32[1,8192,512]{1,2,0:T(8,128)} %stack.20) | data formatting | bytes 33554432 | tf_op jit(solution)/shard_map/stack | solution.py:68
  407.4 33.2 %pad_maximum_fusion = f32[2,8192,512]{2,0,1:T(2,128)} fusion(f32[1,8192,512]{2,0,1:T(1,128)} %copy.117, f32[1,8192,512]{2,0,1:T(1,128)} %copy.116), kind=kLoop, calls=%fused_computation.2 | loop fusion | flops 8388608 | bytes 67108864 | tf_op jit(solution)/shard_map/stack | solution.py:68
  440.7 7.8 all-to-all-start
  449.6 748.2 %all-to-all-done = f32[2,8192,512]{2,0,1:T(2,128)} async-done(((f32[2,8192,512]{2,0,1:T(2,128)}), f32[2,8192,512]{2,0,1:T(2,128)}, u32[]{:S(2)}, u32[]{:S(2)}) %all-to-all-start) | async-done | bytes 33554464 | tf_op jit(solution)/shard_map/all_to_all | solution.py:180
  1197.8 31.8 %copy.249 = f32[2,32,256,512]{3,1,2,0:T(8,128)} copy(f32[2,32,256,512]{3,0,2,1:T(2,128)} %bitcast.17) | data formatting | bytes 67108864 | tf_op jit(solution)/shard_map/all_to_all | solution.py:180
  1229.6 21.5 fusion.4
  1251.1 21.7 fusion.5
  1272.8 24.3 %fusion.24 = f32[32,256,512]{2,0,1:T(8,128)} fusion(f32[32,256,512]{2,0,1:T(8,128)} %fusion.5, f32[2,256,32,512]{3,2,1,0:T(8,128)} %bitcast.203), kind=kOutput, calls=%fused_computation.41 | convolution fusion | flops 1614821376 | bytes 50331648 | tf_op jit(solution)/shard_map/tpn,pk->tkn/dot_general | solution.py:22
  1297.1 32.8 %subtract_bitcast_fusion.2 = (f32[256,32,512]{2,1,0:T(8,128)}, f32[256,32,512]{2,1,0:T(8,128)}) fusion(f32[32,256,512]{2,0,1:T(8,128)} %fusion.24, f32[32,512]{1,0:T(8,128)S(1)} %get-tuple-element.49, f32[32,512]{1,0:T(8,128)S(1)} %get-tuple-element.50, f32[32,256,512]{2,0,1:T(8,128)} %fusion.4, f32[2,256,32,512]{3,2,1,0:T(8,128)} %bitcast.204), kind=kOutput, calls=%fused_computation.16 | convolution fusion | flops 1639987200 | bytes 84017152 | tf_op jit(solution)/shard_map/tpn,pk->tkn/dot_general | solution.py:22
  1329.9 63.2 %fusion.8 = f32[512,256,32]{1,0,2:T(8,128)} fusion(f32[256,32,512]{2,1,0:T(8,128)} %get-tuple-element.12), kind=kOutput, calls=%fused_computation.24 | convolution fusion | flops 25773473792 | bytes 33554432 | tf_op jit(solution)/shard_map/tkn,nj->tjk/dot_general | solution.py:22
  1393.1 51.3 %fusion.10 = f32[512,256,32]{1,0,2:T(8,128)} fusion(f32[256,32,512]{2,1,0:T(8,128)S(1)} %copy-done), kind=kOutput, calls=%fused_computation.26 | convolution fusion | flops 25773473792 | bytes 33554432 | tf_op jit(solution)/shard_map/tkn,nj->tjk/dot_general | solution.py:22
  1444.4 64.2 %subtract_bitcast_fusion.1 = f32[256,512,32]{0,1,2:T(8,128)} fusion(f32[512,256,32]{1,0,2:T(8,128)} %fusion.10, f32[256,32,512]{2,1,0:T(8,128)} %get-tuple-element.11), kind=kOutput, calls=%fused_computation.14 | convolution fusion | flops 25777668096 | bytes 50331648 | tf_op jit(solution)/shard_map/tkn,nj->tjk/dot_general | solution.py:22
  1508.6 64.1 %add_bitcast_fusion.1 = f32[256,512,32]{0,1,2:T(8,128)} fusion(f32[512,256,32]{1,0,2:T(8,128)} %fusion.8, f32[256,32,512]{2,1,0:T(8,128)} %get-tuple-element.11), kind=kOutput, calls=%fused_computation.13 | convolution fusion | flops 25777668096 | bytes 50331648 | tf_op jit(solution)/shard_map/tkn,nj->tjk/dot_general | solution.py:22
  1572.8 17.9 copy.126
  1590.7 21.0 copy.122
  1611.7 32.5 %broadcast_multiply_fusion.1 = (f32[1,256,16,1024]{1,3,2,0:T(8,128)}, f32[1,256,16,1024]{1,3,2,0:T(8,128)}, f32[1,256,16,1024]{1,3,2,0:T(8,128)}, f32[1,256,16,1024]{1,3,2,0:T(8,128)}) fusion(f32[16,1024]{1,0:T(8,128)S(1)} %get-tuple-element.51, f32[1,256,16,1024]{1,3,2,0:T(8,128)} %bitcast.209, pred[16,1024]{1,0:T(8,128)(4,1)S(1)} %fusion.134, ...), kind=kLoop, calls=%fused_computation.44 | loop fusion | flops 46137344 | bytes 100811776 | tf_op jit(solution)/shard_map/mul | solution.py:183
  1644.2 21.9 broadcast_multiply_fusion.3
  1666.1 20.0 maximum_reduce_fusion.1
  1698.3 19.8 maximum_reduce_fusion
  1763.1 9.4 copy.137
  1777.4 185.1 %all-to-all-done.1 = f32[3,1024,512]{2,0,1:T(4,128)} async-done(((f32[3,1024,512]{2,0,1:T(4,128)}), f32[3,1024,512]{2,0,1:T(4,128)}, u32[]{:S(2)}, u32[]{:S(2)}) %all-to-all-start.1) | async-done | bytes 6291488 | tf_op jit(solution)/shard_map/all_to_all | solution.py:188
  1962.5 8.1 copy.138
  1970.6 8.2 reshape.773
  1978.8 12.1 fusion.345
  1994.2 10.6 fusion.92
  2004.8 19.4 stack.27
  2024.2 19.7 stack.26
  2044.0 6.8 broadcast_multiply_fusion.4
  2050.8 12.6 fusion.40
  2063.3 12.9 fusion.42
  2076.2 12.5 fusion.44
  2088.7 12.7 fusion.46
  2101.4 22.6 %fusion.16 = f32[256,5,32,64]{0,3,2,1:T(8,128)} fusion(f32[256,64]{0,1:T(8,128)S(1)} %get-tuple-element.55, f32[256,64]{0,1:T(8,128)S(1)} %get-tuple-element.56, f32[5,32,256,64]{2,3,1,0:T(8,128)} %fusion.44, f32[5,32,256,64]{2,3,1,0:T(8,128)} %fusion.40, f32[5,32,256,64]{2,3,1,0:T(8,128)} %fusion.46, f32[5,32,256,64]{2,3,1,0:T(8,128)} %fusion.42), kind=kOutput, calls=%fused_computation.33 | convolution fusion | flops 8067088384 | bytes 52559872 | tf_op jit(solution)/shard_map/fytu,tv->fyvu/dot_general | solution.py:22
  2124.0 24.9 %subtract_bitcast_fusion.4 = f32[5,32,256,64]{2,3,1,0:T(8,128)} fusion(f32[256,5,32,64]{0,3,2,1:T(8,128)} %fusion.16, f32[256,64]{0,1:T(8,128)S(1)} %get-tuple-element.55, f32[256,64]{0,1:T(8,128)S(1)} %get-tuple-element.56, f32[5,32,256,64]{2,3,1,0:T(8,128)} %fusion.44, f32[5,32,256,64]{2,3,1,0:T(8,128)} %fusion.40, f32[5,32,256,64]{2,3,1,0:T(8,128)} %fusion.46, ...), kind=kOutput, calls=%fused_computation.32 | convolution fusion | flops 8069709824 | bytes 63045632 | tf_op jit(solution)/shard_map/fytu,tv->fyvu/dot_general | solution.py:22
  2148.9 8.2 fusion.344
  (71 shorter events, 118.1 us)
Async XLA Ops:
  440.7 757.1 %all-to-all-start = ((f32[2,8192,512]{2,0,1:T(2,128)}), f32[2,8192,512]{2,0,1:T(2,128)}, u32[]{:S(2)}, u32[]{:S(2)}) async-start(f32[2,8192,512]{2,0,1:T(2,128)} %pad_maximum_fusion), calls=%async_computation | async-start | bytes 67108864 | tf_op jit(solution)/shard_map/all_to_all | solution.py:180
  1329.9 63.2 %copy-start = (f32[256,32,512]{2,1,0:T(8,128)S(1)}, f32[256,32,512]{2,1,0:T(8,128)}, u32[]{:S(2)}) copy-start(f32[256,32,512]{2,1,0:T(8,128)} %get-tuple-element.12) | copy-start | bytes 50331652
  1508.6 82.1 %slice-start = ((s8[16777216]{0:T(1024)(128)(4,1)}), s8[4194304]{0:T(1024)(128)(4,1)S(1)}, s32[]{:S(2)}) async-start(s8[16777216]{0:T(1024)(128)(4,1)} %bitcast.205), calls=%async_computation.2 | async-start | bytes 8388608
  1508.6 82.0 %slice-start.1 = ((s8[16777216]{0:T(1024)(128)(4,1)}), s8[4194304]{0:T(1024)(128)(4,1)S(1)}, s32[]{:S(2)}) async-start(s8[16777216]{0:T(1024)(128)(4,1)} %bitcast.205), calls=%async_computation.3 | async-start | bytes 8388608
  1508.6 82.0 %slice-start.2 = ((s8[16777216]{0:T(1024)(128)(4,1)}), s8[4194304]{0:T(1024)(128)(4,1)S(1)}, s32[]{:S(2)}) async-start(s8[16777216]{0:T(1024)(128)(4,1)} %bitcast.205), calls=%async_computation.4 | async-start | bytes 8388608
  1572.8 17.9 slice-start.3
  1698.3 26.5 %copy-start.5 = (f32[32,32]{0,1:T(8,128)S(1)}, f32[32,32]{0,1:T(8,128)}, u32[]{:S(2)}) copy-start(f32[32,32]{0,1:T(8,128)} %get-tuple-element.53) | copy-start | bytes 12292
  1698.3 26.5 %copy-start.6 = (f32[32,32]{0,1:T(8,128)S(1)}, f32[32,32]{0,1:T(8,128)}, u32[]{:S(2)}) copy-start(f32[32,32]{0,1:T(8,128)} %get-tuple-element.54) | copy-start | bytes 12292
  1718.1 6.7 copy-start.3
  1772.5 190.0 %all-to-all-start.1 = ((f32[3,1024,512]{2,0,1:T(4,128)}), f32[3,1024,512]{2,0,1:T(4,128)}, u32[]{:S(2)}, u32[]{:S(2)}) async-start(f32[3,1024,512]{2,0,1:T(4,128)} %copy.137), calls=%async_computation.1 | async-start | bytes 16777216 | tf_op jit(solution)/shard_map/all_to_all | solution.py:188
  2193.7 5.5 copy-start.2
  2193.7 8.5 slice-start.4
  2196.3 5.9 slice-start.5
  2199.3 3.7 slice-start.6
  2199.3 4.3 copy-start.1
  2204.5 4.8 copy-start.4
where the time goes:
time: 2220 us; the launch traced here: 2210 us
  waiting for transfers between devices  933 us (42%)
  matrix products  670 us (30%)
  local copies, waits for them, and re-layouts  423 us (19%)
  other arithmetic  170 us (8%)
    all_to_all x1, waiting for transfers between devices, body(): lax.all_to_all(spectrum, ('row', 'col'), split_axis=1, concat_axis=2, til...  748 us
    dot_general x26, matrix products, product(): jnp.einsum(form, left, right, precision=HIGHEST, preferred_element_type=j...  588 us
    all_to_all x1, waiting for transfers between devices, body(): lax.all_to_all(outgoing, ('row', 'col'), split_axis=1, concat_axis=2, til...  185 us
    another operation x4, local copies, waits for them, and re-layouts, column_spectrum(): return jnp.stack([real, imaginary]).reshape(2, devices * block, rows_dev)  106 us
    dot_general x2, matrix products, product_input(): jnp.einsum(form, left, right, precision=SPLIT_THREE, preferred_element_ty...  82 us
  transfers between devices with their start and end apart: 2, of which 2 were waited for; matrix products, arithmetic and copies ran while one was open for 0% of the time, Pallas kernels for 0%

commit v1 on v0

v1 whole, which is shorter than its diff:
```python
import functools
import math

import jax
import jax.numpy as jnp
import numpy as np
from jax import lax
from jax.experimental import pallas as pl
from jax.experimental.pallas import tpu as pltpu
from jax.sharding import PartitionSpec as P

STRIDE = 16
LANES = 128
TILE = 8
VMEM = 56 * 2**20
F32 = jnp.float32
BF16 = jnp.bfloat16


def plus(a, b):
    return b if a is None else a if b is None else a + b


def minus(a, b):
    return a if b is None else -b if a is None else a - b


def turned(value, numerator, denominator):
    numerator %= denominator
    real, imaginary = value
    eighth = 8 * numerator / denominator
    if eighth == 0:
        return value
    if eighth == 2:
        return (None if imaginary is None else -imaginary, real)
    if eighth == 4:
        return (-real, None if imaginary is None else -imaginary)
    if eighth == 6:
        return (imaginary, None if real is None else -real)
    cosine = math.cos(2 * math.pi * numerator / denominator)
    sine = math.sin(2 * math.pi * numerator / denominator)
    if real is None:
        return (imaginary * -sine, imaginary * cosine)
    if imaginary is None:
        return (real * cosine, real * sine)
    if eighth in (1, 3, 5, 7):
        scale = math.sqrt(0.5)
        if eighth == 1:
            return ((real - imaginary) * scale, (real + imaginary) * scale)
        if eighth == 3:
            return ((real + imaginary) * -scale, (real - imaginary) * scale)
        if eighth == 5:
            return ((imaginary - real) * scale, (real + imaginary) * -scale)
        return ((real + imaginary) * scale, (imaginary - real) * scale)
    return (real * cosine - imaginary * sine, real * sine + imaginary * cosine)


def c_add(a, b):
    return (plus(a[0], b[0]), plus(a[1], b[1]))


def c_sub(a, b):
    return (minus(a[0], b[0]), minus(a[1], b[1]))


def conj(a):
    return (a[0], None if a[1] is None else -a[1])


def fft_complex(values):
    count = len(values)
    if count == 1:
        return list(values)
    even, odd = fft_complex(values[0::2]), fft_complex(values[1::2])
    out = [None] * count
    for k in range(count // 2):
        term = turned(odd[k], -k, count)
        out[k] = c_add(even[k], term)
        out[k + count // 2] = c_sub(even[k], term)
    return out


def fft_real(values):
    count = len(values)
    if count == 1:
        return [(values[0], None)]
    if count == 2:
        return [(values[0] + values[1], None), (values[0] - values[1], None)]
    even, odd = fft_real(values[0::2]), fft_real(values[1::2])
    out = [None] * (count // 2 + 1)
    for k in range(count // 4 + 1):
        term = turned(odd[k], -k, count)
        out[k] = c_add(even[k], term)
        if k < count // 4:
            low = c_sub(even[k], term)
            real, imaginary = low
            if imaginary is not None:
                imaginary = term[1] - even[k][1] if even[k][1] is not None else term[1]
            out[count // 2 - k] = (real, imaginary)
    return out


def ifft_real(values, count):
    if count == 2:
        return [values[0][0] + values[1][0], values[0][0] - values[1][0]]
    even, odd = [], []
    for k in range(count // 4 + 1):
        a, b = values[k], values[count // 2 - k]
        if k == count // 4:
            even.append((a[0] + a[0], None))
            odd.append((-(a[1] + a[1]), None))
        elif k == 0:
            even.append((a[0] + b[0], None))
            odd.append((a[0] - b[0], None))
        else:
            even.append((a[0] + b[0], a[1] - b[1]))
            odd.append(turned((a[0] - b[0], a[1] + b[1]), k, count))
    out = [None] * count
    out[0::2] = ifft_real(even, count // 2)
    out[1::2] = ifft_real(odd, count // 2)
    return out


def halves(table):
    table = np.asarray(table, np.float32)
    high = table.astype(jnp.bfloat16)
    low = (table - high.astype(np.float32)).astype(jnp.bfloat16)
    return high, low


def column_bins(length):
    groups = length // LANES
    slot = np.arange(groups // 2)[:, None]
    lane = np.arange(LANES)[None, :]
    bins = slot + groups * lane
    bins = np.where(bins >= length // 2, bins - length, bins)
    half = LANES // 2
    bins[0] = np.where(lane[0] < half, groups * lane[0], groups // 2 + groups * (lane[0] - half))
    return bins


def column_table(length):
    bins = column_bins(length)
    slots = bins.shape[0]
    angle = 2 * np.pi / length * (bins[:, None, :] * np.arange(LANES)[None, :, None] % length)
    cosine, sine = np.cos(angle), np.sin(angle)
    table = np.zeros((slots, 2 * LANES, 2 * LANES))
    table[:, :LANES, :LANES] = cosine
    table[:, :LANES, LANES:] = -sine
    table[:, LANES:, :LANES] = sine
    table[:, LANES:, LANES:] = cosine
    half = LANES // 2
    first = np.zeros((2 * LANES, 2 * LANES))
    for begin, rows in ((0, slice(0, LANES)), (half, slice(LANES, 2 * LANES))):
        lanes = slice(begin, begin + half)
        first[rows, begin : begin + half] = cosine[0][:, lanes]
        first[rows, LANES + begin : LANES + begin + half] = -sine[0][:, lanes]
    table[0] = first
    high, low = halves(table)
    return np.concatenate([high, low], axis=1)


def ray_tables(rays, plane_rays, length):
    pairs = rays // 2
    rows = pairs + TILE
    order = np.arange(rows)
    angle = 2 * np.pi / rays * (order[:, None] * np.arange(plane_rays)[None, :] % rays)
    keep = (order <= pairs)[:, None]
    forward = np.concatenate([np.where(keep, np.cos(angle), 0), np.where(keep, -np.sin(angle), 0)])
    high, low = halves(forward)
    forward = np.concatenate([high, low, high], axis=1)
    turn = 2 * np.pi / length * (order[:, None] * np.arange(STRIDE)[None, :] % length)
    twist = np.zeros((rows, LANES), np.float32)
    twist[:, :STRIDE] = np.cos(turn)
    twist[:, STRIDE : 2 * STRIDE] = -np.sin(turn)
    angle = 2 * np.pi / rays * (np.arange(rays)[:, None] * np.arange(pairs)[None, :] % rays)
    cosine = np.cos(angle)
    cosine[:, 0] = 0.5
    backward = np.concatenate([cosine, np.sin(angle)], axis=1)
    high, low = halves(backward)
    return forward, twist, np.concatenate([high, low], axis=1)


def split(value):
    high = value.astype(BF16)
    return high, (value - high.astype(F32)).astype(BF16)


def dot(left, right):
    return jnp.dot(left, right, preferred_element_type=F32)


def params():
    return pltpu.CompilerParams(vmem_limit_bytes=VMEM)


def groups_kernel(x_ref, y_ref, sum_ref):
    rows, length = x_ref.shape
    groups = length // LANES

    @pl.when(pl.program_id(0) == 0)
    def _():
        sum_ref[...] = jnp.zeros_like(sum_ref)

    def step(index, carry):
        first = pl.multiple_of(index * 2 * TILE, 2 * TILE)
        for half in range(2):
            blocks = []
            for u in range(groups):
                lanes = slice(u * LANES, (u + 1) * LANES)
                block = x_ref[pl.ds(first, 2 * TILE), lanes].astype(F32)
                block = block[half * TILE : (half + 1) * TILE]
                sum_ref[:, lanes] += block
                blocks.append(block)
            bins = fft_real(blocks)
            place = pl.ds(pl.multiple_of(first + half * TILE, TILE), TILE)
            for slot in range(groups // 2):
                real, imaginary = bins[slot]
                if slot == 0:
                    imaginary = bins[groups // 2][0]
                y_ref[slot, 0, place] = real
                y_ref[slot, 1, place] = imaginary
        return carry

    lax.fori_loop(0, rows // (2 * TILE), step, 0)


def over_groups(field):
    rows, length = field.shape
    slots = length // LANES // 2
    step = min(rows, 32)
    return pl.pallas_call(
        groups_kernel,
        grid=(rows // step,),
        in_specs=[pl.BlockSpec((step, length), lambda i: (i, 0))],
        out_specs=[
            pl.BlockSpec((slots, 2, step, LANES), lambda i: (0, 0, i, 0)),
            pl.BlockSpec((TILE, length), lambda i: (0, 0)),
        ],
        out_shape=[
            jax.ShapeDtypeStruct((slots, 2, rows, LANES), F32),
            jax.ShapeDtypeStruct((TILE, length), F32),
        ],
        compiler_params=params(),
        cost_estimate=pl.CostEstimate(
            flops=20 * rows * length, bytes_accessed=6 * rows * length, transcendentals=0
        ),
        name="column_groups",
    )(field)


def lanes_kernel(y_ref, table_ref, out_ref):
    own = y_ref.shape[2] // STRIDE
    sides = []
    for side in range(2):
        pieces = [y_ref[0, side, pl.ds(s, own, stride=STRIDE), :] for s in range(STRIDE)]
        whole = jnp.concatenate(pieces, axis=0)
        sides.append(whole)
    high, low = split(jnp.concatenate(sides, axis=1))
    table = table_ref[0]
    top, rest = table[: 2 * LANES], table[2 * LANES :]
    out_ref[0, 0] = dot(
        jnp.concatenate([high, high, low], axis=1), jnp.concatenate([top, rest, top], axis=0)
    )


def over_lanes(grouped, table, devices, begin, count):
    slots, _, rows, lanes = grouped.shape
    width = 2 * lanes
    owned = slots // devices
    return pl.pallas_call(
        lanes_kernel,
        grid=(devices, count),
        in_specs=[
            pl.BlockSpec(
                (1, 2, rows, lanes), lambda d, i: (d * owned + begin + i, 0, 0, 0)
            ),
            pl.BlockSpec((1, 2 * width, width), lambda d, i: (d * owned + begin + i, 0, 0)),
        ],
        out_specs=pl.BlockSpec((1, 1, rows, width), lambda d, i: (d, i, 0, 0)),
        out_shape=jax.ShapeDtypeStruct((devices, count, rows, width), F32),
        compiler_params=params(),
        cost_estimate=pl.CostEstimate(
            flops=6 * devices * count * rows * width * width,
            bytes_accessed=8 * devices * count * rows * width,
            transcendentals=0,
        ),
        name="column_lanes",
    )(grouped, table)


def rays_kernel(has_mean, place_ref, mean_ref, x_ref, forward_ref, twist_ref, backward_ref, out_ref, cos_ref, sin_ref,
                pq_ref, ab_ref, high_ref, low_ref):
    sources, _, _, own, width = x_ref.shape
    planes = out_ref.shape[0]
    plane_rays = sources * own
    rays = planes * plane_rays
    pairs = rays // 2
    rows = pairs + TILE
    length = rays * STRIDE
    half = length // 2
    groups = length // LANES

    @pl.when(pl.program_id(0) == 0)
    def _():
        for s in range(STRIDE):
            cos_ref[s] = jnp.broadcast_to(twist_ref[:, s : s + 1], (rows, LANES))
            sin_ref[s] = jnp.broadcast_to(
                twist_ref[:, STRIDE + s : STRIDE + s + 1], (rows, LANES)
            )

    if has_mean:
        at_mean = lax.broadcasted_iota(jnp.int32, (1, width), 1) == 0
        at_mean = jnp.logical_and(at_mean, place_ref[1] + pl.program_id(0) == 0)
        offset = jnp.where(at_mean, mean_ref[0] * float(length), 0.0)

    def forward(s, carry):
        value = x_ref[:, 0, s].reshape(plane_rays, width)
        if has_mean:
            value = value - offset
        high, low = split(value)
        pq_ref[s] = dot(forward_ref[...], jnp.concatenate([high, high, low], axis=0))
        return carry

    lax.fori_loop(0, STRIDE, forward, 0)

    slot = place_ref[1] + pl.program_id(0)
    lane = lax.broadcasted_iota(jnp.int32, (TILE, LANES), 1)
    bins = slot + groups * lane
    bins = jnp.where(bins >= half, bins - length, bins)
    middle = LANES // 2
    first = jnp.where(lane < middle, groups * lane, groups // 2 + groups * (lane - middle))
    bins = jnp.where(slot == 0, first, bins).astype(F32)
    bins_squared = bins * bins
    sublane = lax.broadcasted_iota(jnp.int32, (TILE, LANES), 0)

    def filtered(block, carry):
        base = pl.multiple_of(block * TILE, TILE)
        at_p = pl.ds(base, TILE)
        at_q = pl.ds(pl.multiple_of(rows + base, TILE), TILE)
        order = (sublane + base).astype(F32)
        weights, wave_weights = [], []
        for a in range(STRIDE):
            wave = order + float(a * rays - (length if a >= STRIDE // 2 else 0))
            squared = wave * wave + bins_squared
            if a == 0:
                squared_safe = jnp.where(squared > 0.0, squared, 1.0)
            else:
                squared_safe = squared
            inverse = pl.reciprocal(squared_safe, approx=True)
            inverse = inverse * (2.0 - squared_safe * inverse)
            inverse = inverse * (2.0 - squared_safe * inverse)
            if a == 0:
                inverse = jnp.where(squared > 0.0, inverse, 0.0)
            if a == STRIDE // 2:
                inverse = jnp.where(order > 0.0, inverse, 0.0)
            weights.append(inverse)
            wave_weights.append(inverse * wave)
        sums = []
        for side in range(2):
            values = []
            for s in range(STRIDE):
                pr, pi = pq_ref[s, at_p, :LANES], pq_ref[s, at_p, LANES:]
                qr, qi = pq_ref[s, at_q, :LANES], pq_ref[s, at_q, LANES:]
                real, imaginary = (pr - qi, pi + qr) if side == 0 else (pr + qi, qr - pi)
                if s > 0:
                    cosine, sine = cos_ref[s, at_p], sin_ref[s, at_p]
                    real, imaginary = (
                        real * cosine - imaginary * sine,
                        real * sine + imaginary * cosine,
                    )
                values.append((real, imaginary))
            spectrum = fft_complex(values)
            for chosen in (weights, wave_weights):
                for which in range(2):
                    total = spectrum[0][which] * chosen[0]
                    for a in range(1, STRIDE):
                        total = total + spectrum[a][which] * chosen[a]
                    sums.append(total)
        a0r, a0i, a1r, a1i, b0r, b0i, b1r, b1i = sums
        even = (a0r + b0r, a0i - b0i, a1r - b1r, a1i + b1i)
        odd = (a0r - b0r, a0i + b0i, a1r + b1r, a1i - b1i)
        for index, value in enumerate(even):
            ab_ref[0, at_p, index * LANES : (index + 1) * LANES] = value
        for index, value in enumerate((-odd[1], odd[0], -odd[3], odd[2])):
            ab_ref[1, at_p, index * LANES : (index + 1) * LANES] = value
        return carry

    lax.fori_loop(0, rows // TILE, filtered, 0)

    for side in range(2):
        high, low = split(ab_ref[side, :pairs])
        high_ref[side * pairs : (side + 1) * pairs] = high
        low_ref[side * pairs : (side + 1) * pairs] = low
    last = ab_ref[0, pairs : pairs + TILE][:1] * 0.5
    parity = lax.broadcasted_iota(jnp.int32, (plane_rays, 4 * LANES), 0) % 2
    tail = jnp.where(parity == 0, last, -last)

    def backward(shift, carry):
        at = pl.ds(pl.multiple_of(shift * plane_rays, plane_rays), plane_rays)
        total = dot(backward_ref[at, :rays], high_ref[...])
        total += dot(backward_ref[at, rays:], high_ref[...])
        total += dot(backward_ref[at, :rays], low_ref[...])
        plane = lax.rem(place_ref[0] + shift, planes)
        out_ref[plane, :, 0] = (total + tail).reshape(sources, own, 4 * LANES)
        return carry

    lax.fori_loop(0, planes, backward, 0)


def to_rays(place, mean, arrived, tables, planes):
    sources, count, strides, own, width = arrived.shape
    forward, twist, backward = tables
    rays = planes * sources * own
    rows = rays // 2 + TILE

    def whole(array):
        return pl.BlockSpec(
            array.shape, lambda i, place: (0, 0), pipeline_mode=pl.Buffered(1)
        )

    return pl.pallas_call(
        functools.partial(rays_kernel, mean is not None),
        grid_spec=pltpu.PrefetchScalarGridSpec(
            num_scalar_prefetch=1,
            grid=(count,),
            in_specs=[
                pl.BlockSpec(memory_space=pltpu.SMEM),
                pl.BlockSpec(
                    (sources, 1, strides, own, width), lambda i, place: (0, i, 0, 0, 0)
                ),
                whole(forward),
                whole(twist),
                whole(backward),
            ],
            out_specs=pl.BlockSpec(
                (planes, sources, 1, own, 4 * LANES), lambda i, place: (0, 0, i, 0, 0)
            ),
            scratch_shapes=[
                pltpu.VMEM((STRIDE, rows, LANES), F32),
                pltpu.VMEM((STRIDE, rows, LANES), F32),
                pltpu.VMEM((STRIDE, 2 * rows, width), F32),
                pltpu.VMEM((2, rows, 4 * LANES), F32),
                pltpu.VMEM((rays, 4 * LANES), BF16),
                pltpu.VMEM((rays, 4 * LANES), BF16),
            ],
        ),
        out_shape=jax.ShapeDtypeStruct((planes, sources, count, own, 4 * LANES), F32),
        compiler_params=params(),
        cost_estimate=pl.CostEstimate(
            flops=8 * count * (6 * STRIDE * 2 * rows * sources * own * width
                           + 6 * rays * rays * 4 * LANES),
            bytes_accessed=4 * arrived.size + 16 * count * rays * LANES,
            transcendentals=0,
        ),
        name="ray_rows",
    )(place, jnp.zeros(1, F32) if mean is None else mean, arrived, forward, twist, backward)


def back_kernel(t_ref, table_ref, factor_ref, out_ref):
    t = t_ref[0, 0]
    t0r, t0i, t1r, t1i = (t[:, n * LANES : (n + 1) * LANES] for n in range(4))
    factor = factor_ref[0]
    by_r, by_c, by_cc, by_rc = (factor[n : n + 1] for n in range(4))
    real = jnp.concatenate([-t1i * by_r, -t0i * by_c, t0r * by_cc, t1r * by_rc], axis=0)
    imaginary = jnp.concatenate([t1r * by_r, t0r * by_c, t0i * by_cc, t1i * by_rc], axis=0)
    high, low = split(jnp.concatenate([real, imaginary], axis=1))
    table = table_ref[0]
    top, rest = table[: 2 * LANES], table[2 * LANES :]
    form = (((1,), (1,)), ((), ()))
    total = lax.dot_general(high, top, form, preferred_element_type=F32)
    total += lax.dot_general(high, rest, form, preferred_element_type=F32)
    total += lax.dot_general(low, top, form, preferred_element_type=F32)
    out_ref[0, 0] = total.reshape(out_ref.shape[2:])


def field_factors(length):
    bins = column_bins(length).astype(np.float64)
    wave = 2 * np.pi / length
    scale = -2.0 / (4 * np.pi**2)
    weight = np.ones_like(bins)
    weight[0] = 2.0
    weight[0, 0] = 1.0
    factor = np.zeros((bins.shape[0], TILE, LANES))
    factor[:, 0] = scale * wave * weight
    factor[:, 1] = scale * wave * bins * weight
    factor[:, 2] = -scale * wave * wave * bins * bins * weight
    factor[:, 3] = -scale * wave * wave * bins * weight
    return factor.astype(np.float32)


def back_over_lanes(returned, table, factors, begin):
    devices, count, own, width = returned.shape
    owned = table.shape[0] // devices
    slot = lambda d, i: (d * owned + begin + i, 0, 0)
    return pl.pallas_call(
        back_kernel,
        grid=(devices, count),
        in_specs=[
            pl.BlockSpec((1, 1, own, width), lambda d, i: (d, i, 0, 0)),
            pl.BlockSpec((1,) + table.shape[1:], slot),
            pl.BlockSpec((1,) + factors.shape[1:], slot),
        ],
        out_specs=pl.BlockSpec((1, 1, 4, own, 2 * LANES), lambda d, i: (d, i, 0, 0, 0)),
        out_shape=jax.ShapeDtypeStruct((devices, count, 4, own, 2 * LANES), F32),
        compiler_params=params(),
        cost_estimate=pl.CostEstimate(
            flops=6 * devices * count * 4 * own * 4 * LANES * LANES,
            bytes_accessed=devices * count * (12 * own * width + 8 * LANES * LANES),
            transcendentals=0,
        ),
        name="fields_lanes",
    )(returned, table, factors)


def advance_kernel(weight_ref, *refs):
    parts, (base_ref, state_ref, out_ref, field_ref) = refs[:-4], refs[-4:]
    devices = parts[0].shape[0]
    length = base_ref.shape[1]
    groups = length // LANES
    places = [
        (part, device, index)
        for device in range(devices)
        for part in parts
        for index in range(part.shape[1])
    ]

    def transform(field, carry):
        bins = []
        for part, device, index in places:
            bins.append(
                (part[device, index, field, :, :LANES], part[device, index, field, :, LANES:])
            )
        bins.append((bins[0][1], None))
        bins[0] = (bins[0][0], None)
        for u, block in enumerate(ifft_real(bins, groups)):
            field_ref[field, :, u * LANES : (u + 1) * LANES] = block
        return carry

    lax.fori_loop(0, 4, transform, 0)
    weight = weight_ref[0]

    def step(u, carry):
        at = pl.ds(pl.multiple_of(u * LANES, LANES), LANES)
        alpha_r, alpha_c, cc, rc = (field_ref[n, :, at] for n in range(4))
        rr = base_ref[:, at] - cc
        rr, cc, rc = weight * rr, weight * cc, weight * rc
        ul, ur, ll, lr = (state_ref[n, :, at] for n in range(2, 6))
        out_ref[0, :, at] = state_ref[0, :, at] - weight * alpha_r
        out_ref[1, :, at] = state_ref[1, :, at] - weight * alpha_c
        out_ref[2, :, at] = ul - (rr * ul + rc * ll)
        out_ref[3, :, at] = ur - (rr * ur + rc * lr)
        out_ref[4, :, at] = ll - (rc * ul + cc * ll)
        out_ref[5, :, at] = lr - (rc * ur + cc * lr)
        return carry

    lax.fori_loop(0, groups, step, 0)


def advance(weight, parts, base, state):
    devices, _, fields, own, width = parts[0].shape
    length = base.shape[1]
    return pl.pallas_call(
        advance_kernel,
        grid=(own // TILE,),
        in_specs=[pl.BlockSpec(memory_space=pltpu.SMEM)]
        + [
            pl.BlockSpec(
                (devices, part.shape[1], fields, TILE, width), lambda i: (0, 0, 0, i, 0)
            )
            for part in parts
        ]
        + [
            pl.BlockSpec((TILE, length), lambda i: (i, 0)),
            pl.BlockSpec((6, TILE, length), lambda i: (0, i, 0)),
        ],
        out_specs=pl.BlockSpec((6, TILE, length), lambda i: (0, i, 0)),
        out_shape=jax.ShapeDtypeStruct((6, own, length), F32),
        scratch_shapes=[pltpu.VMEM((fields, TILE, length), F32)],
        compiler_params=params(),
        cost_estimate=pl.CostEstimate(
            flops=100 * own * length, bytes_accessed=72 * own * length, transcendentals=0
        ),
        name="ray_step",
    )(weight, *parts, base, state)


def column_totals(sums):
    length = sums.shape[1]
    own = jnp.stack([jnp.sum(sums, axis=0), jnp.sum(sums[0::2] - sums[1::2], axis=0)])
    return lax.psum(own, ("row", "col")) / length


def curvature_sum(field, totals):
    rows, length = field.shape
    sign = jnp.where(jnp.arange(length) % 2 == 0, 1.0, -1.0).astype(F32)
    own = field.reshape(rows // STRIDE, STRIDE, length)[:, 0].astype(F32)
    whole, alternating = totals
    mean = jnp.mean(whole)
    both = jnp.mean(alternating * sign)
    by_row = jnp.mean(own * sign, axis=1, keepdims=True)
    return 2.0 * (own - sign * by_row - alternating + sign * both - mean)


def parted(owned):
    sizes = [1] * owned if owned < 4 else [1] + [2] * (owned // 2 - 1) + [1] * (1 + owned % 2)
    begins = [sum(sizes[:index]) for index in range(len(sizes))]
    return list(zip(begins, sizes))[::-1]


def passed_along(value, axis, steps):
    count = lax.axis_size(axis)
    leading, last = (max(0, -steps), min(count, count - steps))
    return lax.ppermute(value, axis, [(source, source + steps) for source in range(leading, last)])


def body(convergence, lens_weight, rays_in):
    planes = lax.axis_size("row")
    devices = lax.axis_size("col")
    _, rows, length = convergence.shape
    own = rows // STRIDE
    slots = length // LANES // 2
    owned = slots // devices
    runs = parted(owned)
    pieces = len(runs)
    field = convergence[0]
    table = jnp.asarray(column_table(length))
    tables = [jnp.asarray(t) for t in ray_tables(length // STRIDE, own * devices, length)]
    factors = jnp.asarray(field_factors(length))
    grouped, sums = over_groups(field)
    totals = column_totals(sums)
    place = jnp.stack([lax.axis_index("row"), lax.axis_index("col") * owned]).astype(jnp.int32)

    def send(step, *after):
        begin, count = runs[step]
        held = lax.optimization_barrier((grouped, *after))[0]
        return over_lanes(held, table, devices, begin, count)

    def exchange(value):
        return lax.all_to_all(value, "col", split_axis=0, concat_axis=0, tiled=True)

    sent = {step: send(step) for step in range(min(2, pieces))}
    arrived = {}
    for step in range(pieces):
        arrived[step] = exchange(sent[step])
        if step + 2 < pieces:
            sent[step + 2] = send(step + 2, arrived[step])
    summed = {}
    for step, (begin, count) in enumerate(runs):
        held = arrived[step]
        if step + 2 < pieces:
            held = lax.optimization_barrier((held, sent[step + 2]))[0]
        held = held.reshape(devices, count, STRIDE, own, 2 * LANES)
        shift = jnp.asarray(np.array([0, begin], np.int32))
        mean = None
        if begin == 0:
            late = lax.optimization_barrier((totals, arrived[step]))[0]
            mean = jnp.mean(late[0]).reshape(1)
        partial = to_rays(place + shift, mean, held, tables, planes)
        summed[step] = lax.psum_scatter(partial, "row", scatter_dimension=0, tiled=True)[0]
    done = {}
    for step, (begin, _) in enumerate(runs):
        held = summed[step]
        if step == pieces - 1:
            held = lax.optimization_barrier((held, *done.values()))[0]
        done[begin] = back_over_lanes(exchange(held), table, factors, begin)
    parts = [done[begin] for begin in sorted(done)]
    base = curvature_sum(field, late)

    def run_local(start):
        return advance(lens_weight, parts, base, start)[None]

    shell_index = lax.axis_index("shell")
    outputs = run_local(rays_in)
    for group in range(1, lax.axis_size("shell")):
        received = passed_along(outputs[-1], "shell", 1)
        outputs = jnp.where(shell_index == group, run_local(received), outputs)
    return outputs


def solution(mesh):
    in_specs = (P("shell", ("row", "col"), None), P("shell"), P(None, ("row", "col"), None))
    out_specs = P("shell", None, ("row", "col"), None)
    return jax.shard_map(body, mesh=mesh, in_specs=in_specs, out_specs=out_specs, check_vma=False)
```

time: 2220 us -> 644 us (0.29)
  waiting for transfers between devices: 933 us -> 141 us
  matrix products: 670 us -> 0 us
  local copies, waits for them, and re-layouts: 423 us -> 9.86 us
  Pallas kernels: 0 us -> 392 us
  other arithmetic: 170 us -> 8.62 us
  blocking collectives: 0 us -> 33.7 us
  starting transfers between devices: 11.7 us -> 37.1 us
    all_to_all x2 -> x8, waiting for transfers between devices: 933 us -> 141 us  [exchange(): return lax.all_to_all(value, 'col', split_axis=0, concat_axis=0, tiled=True)]
    dot_general x28 -> x0, matrix products: 670 us -> none  [the longest x26 588 us: product(): jnp.einsum(form, left, right, precision=HIGHEST, preferred_element_type=j...]
    pallas_call x0 -> x17, Pallas kernels: none -> 392 us  [the longest x5 235 us: to_rays(): pl.pallas_call(functools.partial(rays_kernel, mean is not None), grid_spe...]
    another operation x8 -> x0, local copies, waits for them, and re-layouts: 176 us -> none  [the longest x4 106 us: column_spectrum(): return jnp.stack([real, imaginary]).reshape(2, devices * block, rows_dev)]
    mul x8 -> x1, other arithmetic: 71.9 us -> 2.71 us  [curvature_sum(): return 2.0 * (own - sign * by_row - alternating + sign * both - mean)]
    sub x3 -> x0, local copies, waits for them, and re-layouts: 57.3 us -> none  [the longest x1 34.5 us: twiddle(): return (real * cosine - imaginary * sine, real * sine + imaginary * cosine)]
    add x3 -> x0, local copies, waits for them, and re-layouts: 54.2 us -> none  [the longest x1 34.5 us: twiddle(): return (real * cosine - imaginary * sine, real * sine + imaginary * cosine)]
    all_to_all x2 -> x0, local copies, waits for them, and re-layouts: 39.9 us -> none  [the longest x1 31.8 us: body(): lax.all_to_all(spectrum, ('row', 'col'), split_axis=1, concat_axis=2, til...]
  transfers between devices with their start and end apart: 2 -> 14, of which waited for: 2 -> 6; matrix products, arithmetic and copies ran while one was open for 0% -> 3% of each run, Pallas kernels for 0% -> 52%
where the time goes in v1:
time: 644 us; the launch traced here: 640 us
  Pallas kernels  392 us (61%)
  waiting for transfers between devices  141 us (22%)
  starting transfers between devices  37.1 us (6%)
  blocking collectives  33.7 us (5%)
  between operations  17.1 us (3%)
  local copies, waits for them, and re-layouts  9.86 us (2%)
  other arithmetic  8.62 us (1%)
    pallas_call x5, Pallas kernels, to_rays(): pl.pallas_call(functools.partial(rays_kernel, mean is not None), grid_spe...  235 us
    all_to_all x8, waiting for transfers between devices, exchange(): return lax.all_to_all(value, 'col', split_axis=0, concat_axis=0, tiled=True)  141 us
    pallas_call x5, Pallas kernels, over_lanes(): pl.pallas_call(lanes_kernel, grid=(devices, count), in_specs=[pl.BlockSpe...  63.5 us
    pallas_call x5, Pallas kernels, back_over_lanes(): pl.pallas_call(back_kernel, grid=(devices, count), in_specs=[pl.BlockSpec...  48.3 us
    all_to_all x8, starting transfers between devices, exchange(): return lax.all_to_all(value, 'col', split_axis=0, concat_axis=0, tiled=True)  36.7 us
    all_to_all x2, blocking collectives, exchange(): return lax.all_to_all(value, 'col', split_axis=0, concat_axis=0, tiled=True)  33.7 us
    pallas_call x1, Pallas kernels, over_groups(): pl.pallas_call(groups_kernel, grid=(rows // step,), in_specs=[pl.BlockSpe...  27.8 us
    pallas_call x1, Pallas kernels, advance(): pl.pallas_call(advance_kernel, grid=(own // TILE,), in_specs=[pl.BlockSpe...  17.2 us
  transfers between devices with their start and end apart: 14, of which 6 were waited for; matrix products, arithmetic and copies ran while one was open for 3% of the time, Pallas kernels for 52%

profile of v1, /device:TPU:0, one launch (start us, length us, event | category | flops | bytes accessed | tf_op | source)
XLA Modules:
  0.0 639.6 jit_solution(18422077159234546382)
XLA Ops:
  7.4 27.8 %column_groups.1 = (f32[64,2,512,128]{3,2,1,0:T(8,128)}, f32[8,16384]{1,0:T(8,128)}) custom-call(bf16[512,16384]{1,0:T(8,128)(2,1)} %bitcast.28), custom_call_target="tpu_custom_call" | custom-call | flops 167772160 | bytes 50331648 | tf_op jit(solution)/shard_map/column_groups/pallas_call | solution.py:232
  35.2 8.4 %column_lanes.5 = f32[8,1,512,256]{3,2,1,0:T(8,128)} custom-call(f32[64,2,512,128]{3,2,1,0:T(8,128)} %get-tuple-element.18.y_ref, bf16[64,512,256]{2,1,0:T(8,128)(2,1)} %constant.71.clone.table_ref), custom_call_target="tpu_custom_call" | custom-call | flops 1610612736 | bytes 8388608 | tf_op jit(solution)/shard_map/column_lanes/pallas_call | solution.py:271
  43.6 5.3 all-to-all-start
  48.9 1.6 slice.13
  50.5 1.6 slice.12
  52.2 0.2 subtract_reduce_fusion
  52.4 0.8 pad_maximum_fusion
  53.2 0.6 iota_add_fusion
  53.8 0.5 copy-done.3
  54.3 0.6 multiply_add_fusion
  54.9 15.6 %column_lanes.8 = f32[8,2,512,256]{3,2,1,0:T(8,128)} custom-call(f32[64,2,512,128]{3,2,1,0:T(8,128)} %get-tuple-element.18.y_ref, bf16[64,512,256]{2,1,0:T(8,128)(2,1)} %constant.71.clone.table_ref), custom_call_target="tpu_custom_call" | custom-call | flops 3221225472 | bytes 16777216 | tf_op jit(solution)/shard_map/column_lanes/pallas_call | solution.py:271
  70.5 27.9 %all-to-all-done = f32[8,1,512,256]{3,2,1,0:T(8,128)} async-done(((f32[8,1,512,256]{3,2,1,0:T(8,128)}), f32[8,1,512,256]{3,2,1,0:T(8,128)}, u32[]{:S(2)}, u32[]{:S(2)}) %all-to-all-start) | async-done | bytes 4194336 | tf_op jit(solution)/shard_map/all_to_all | solution.py:640
  98.4 5.0 all-to-all-start.4
  103.4 15.6 %column_lanes.6 = f32[8,2,512,256]{3,2,1,0:T(8,128)} custom-call(f32[64,2,512,128]{3,2,1,0:T(8,128)} %get-tuple-element.18.y_ref, bf16[64,512,256]{2,1,0:T(8,128)(2,1)} %constant.71.clone.table_ref), custom_call_target="tpu_custom_call" | custom-call | flops 3221225472 | bytes 16777216 | tf_op jit(solution)/shard_map/column_lanes/pallas_call | solution.py:271
  119.0 32.4 %ray_rows.6 = f32[4,8,1,32,512]{4,3,2,1,0:T(8,128)} custom-call(s32[2]{0:T(128)} %get-tuple-element.31.place_ref, f32[1]{0:T(128)} %constant.64.clone.1.mean_ref, f32[8,1,16,32,256]{4,3,2,1,0:T(8,128)} %bitcast.9.x_ref, bf16[1040,768]{1,0:T(8,128)(2,1)} %constant.72.clone.forward_ref, f32[520,128]{1,0:T(8,128)} %constant.73.clone.twist_ref, ...), custom_call_target="tpu_custom_call" | custom-call | flops 78114717696 | bytes 6291456 | tf_op jit(solution)/shard_map/ray_rows/pallas_call | solution.py:422
  151.5 46.3 %all-to-all-done.4 = f32[8,2,512,256]{3,2,1,0:T(8,128)} async-done(((f32[8,2,512,256]{3,2,1,0:T(8,128)}), f32[8,2,512,256]{3,2,1,0:T(8,128)}, u32[]{:S(2)}, u32[]{:S(2)}) %all-to-all-start.4) | async-done | bytes 8388640 | tf_op jit(solution)/shard_map/all_to_all | solution.py:640
  197.8 5.0 all-to-all-start.1
  202.8 15.6 %column_lanes.9 = f32[8,2,512,256]{3,2,1,0:T(8,128)} custom-call(f32[64,2,512,128]{3,2,1,0:T(8,128)} %get-tuple-element.18.y_ref, bf16[64,512,256]{2,1,0:T(8,128)(2,1)} %constant.71.clone.table_ref), custom_call_target="tpu_custom_call" | custom-call | flops 3221225472 | bytes 16777216 | tf_op jit(solution)/shard_map/column_lanes/pallas_call | solution.py:271
  218.4 56.6 %ray_rows.7 = f32[4,8,2,32,512]{4,3,2,1,0:T(8,128)} custom-call(s32[2]{0:T(128)} %get-tuple-element.30.place_ref, f32[1]{0:T(128)} %constant.64.clone.1.mean_ref, f32[8,2,16,32,256]{4,3,2,1,0:T(8,128)} %bitcast.12.x_ref, bf16[1040,768]{1,0:T(8,128)(2,1)} %constant.72.clone.forward_ref, f32[520,128]{1,0:T(8,128)} %constant.73.clone.twist_ref, ...), custom_call_target="tpu_custom_call" | custom-call | flops 156229435392 | bytes 12582912 | tf_op jit(solution)/shard_map/ray_rows/pallas_call | solution.py:422
  275.1 22.0 %all-to-all-done.1 = f32[8,2,512,256]{3,2,1,0:T(8,128)} async-done(((f32[8,2,512,256]{3,2,1,0:T(8,128)}), f32[8,2,512,256]{3,2,1,0:T(8,128)}, u32[]{:S(2)}, u32[]{:S(2)}) %all-to-all-start.1) | async-done | bytes 8388640 | tf_op jit(solution)/shard_map/all_to_all | solution.py:640
  297.1 5.0 all-to-all-start.7
  302.0 0.2 reduce-scatter.12.cloned.1.call-start
  302.2 8.4 %column_lanes.7 = f32[8,1,512,256]{3,2,1,0:T(8,128)} custom-call(f32[64,2,512,128]{3,2,1,0:T(8,128)} %get-tuple-element.18.y_ref, bf16[64,512,256]{2,1,0:T(8,128)(2,1)} %constant.71.clone.table_ref), custom_call_target="tpu_custom_call" | custom-call | flops 1610612736 | bytes 8388608 | tf_op jit(solution)/shard_map/column_lanes/pallas_call | solution.py:271
  310.6 56.8 %ray_rows.8 = f32[4,8,2,32,512]{4,3,2,1,0:T(8,128)} custom-call(s32[2]{0:T(128)} %get-tuple-element.29.place_ref, f32[1]{0:T(128)} %constant.64.clone.1.mean_ref, f32[8,2,16,32,256]{4,3,2,1,0:T(8,128)} %bitcast.14.x_ref, bf16[1040,768]{1,0:T(8,128)(2,1)} %constant.72.clone.forward_ref, f32[520,128]{1,0:T(8,128)} %constant.73.clone.twist_ref, ...), custom_call_target="tpu_custom_call" | custom-call | flops 156229435392 | bytes 12582912 | tf_op jit(solution)/shard_map/ray_rows/pallas_call | solution.py:422
  367.4 28.6 %all-to-all-done.7 = f32[8,2,512,256]{3,2,1,0:T(8,128)} async-done(((f32[8,2,512,256]{3,2,1,0:T(8,128)}), f32[8,2,512,256]{3,2,1,0:T(8,128)}, u32[]{:S(2)}, u32[]{:S(2)}) %all-to-all-start.7) | async-done | bytes 8388640 | tf_op jit(solution)/shard_map/all_to_all | solution.py:640
  396.1 4.6 all-to-all-start.2
  400.7 56.7 %ray_rows.9 = f32[4,8,2,32,512]{4,3,2,1,0:T(8,128)} custom-call(s32[2]{0:T(128)} %get-tuple-element.25.place_ref, f32[1]{0:T(128)} %constant.64.clone.1.mean_ref, f32[8,2,16,32,256]{4,3,2,1,0:T(8,128)} %bitcast.16.x_ref, bf16[1040,768]{1,0:T(8,128)(2,1)} %constant.72.clone.forward_ref, f32[520,128]{1,0:T(8,128)} %constant.73.clone.twist_ref, ...), custom_call_target="tpu_custom_call" | custom-call | flops 156229435392 | bytes 12582912 | tf_op jit(solution)/shard_map/ray_rows/pallas_call | solution.py:422
  457.5 1.0 broadcast_multiply_fusion
  458.5 0.8 fusion.10
  459.9 32.4 %ray_rows.5 = f32[4,8,1,32,512]{4,3,2,1,0:T(8,128)} custom-call(s32[2]{0:T(128)} %copy-done.3, f32[1]{0:T(128)} %bitcast.5.mean_ref, f32[8,1,16,32,256]{4,3,2,1,0:T(8,128)} %bitcast.6.x_ref, bf16[1040,768]{1,0:T(8,128)(2,1)} %constant.72.clone.forward_ref, f32[520,128]{1,0:T(8,128)} %constant.73.clone.twist_ref, bf16[1024,2048]{1,0:T(8,128)(2,1)} %constant.74.clone.backward_ref), custom_call_target="tpu_custom_call" | custom-call | flops 78114717696 | bytes 6291456 | tf_op jit(solution)/shard_map/ray_rows/pallas_call | solution.py:422
  492.4 13.9 %all_to_all.50.t_ref = f32[8,1,32,512]{3,2,1,0:T(8,128)} all-to-all(f32[8,1,32,512]{3,2,1,0:T(8,128)} %bitcast.37), channel_id=1, replica_groups=mesh['shell'=1,'row'=4,'col'=8] {'col'}, dimensions={0} | all-to-all | bytes 1048576 | tf_op jit(solution)/shard_map/all_to_all | solution.py:640
  506.3 19.8 %all_to_all.51.t_ref = f32[8,2,32,512]{3,2,1,0:T(8,128)} all-to-all(f32[8,2,32,512]{3,2,1,0:T(8,128)} %bitcast.32), channel_id=1, replica_groups=mesh['shell'=1,'row'=4,'col'=8] {'col'}, dimensions={0} | all-to-all | bytes 2097152 | tf_op jit(solution)/shard_map/all_to_all | solution.py:640
  526.1 3.6 all-to-all-start.6
  530.3 5.5 slice.16
  535.8 9.2 %all-to-all-done.6.t_ref = f32[8,2,32,512]{3,2,1,0:T(8,128)S(1)} async-done(((f32[8,2,32,512]{3,2,1,0:T(8,128)}), f32[8,2,32,512]{3,2,1,0:T(8,128)S(1)}, u32[]{:S(2)}, u32[]{:S(2)}) %all-to-all-start.6) | async-done | bytes 1048608 | tf_op jit(solution)/shard_map/all_to_all | solution.py:640
  545.0 4.2 all-to-all-start.8
  549.3 6.5 %fields_lanes.5.refs_4_ = f32[8,1,4,32,256]{4,3,2,1,0:T(8,128)} custom-call(f32[8,1,32,512]{3,2,1,0:T(8,128)} %all_to_all.50.t_ref, bf16[64,512,256]{2,1,0:T(8,128)(2,1)} %constant.71.clone.table_ref, f32[64,8,128]{2,1,0:T(8,128)} %constant.75.clone.factor_ref), custom_call_target="tpu_custom_call" | custom-call | flops 402653184 | bytes 2621440 | tf_op jit(solution)/shard_map/fields_lanes/pallas_call | solution.py:496
  555.8 0.6 multiply_reduce_fusion
  557.1 1.2 fusion
  558.3 11.8 %fields_lanes.6.refs_3_ = f32[8,2,4,32,256]{4,3,2,1,0:T(8,128)} custom-call(f32[8,2,32,512]{3,2,1,0:T(8,128)} %all_to_all.51.t_ref, bf16[64,512,256]{2,1,0:T(8,128)(2,1)} %constant.71.clone.table_ref, f32[64,8,128]{2,1,0:T(8,128)} %constant.75.clone.factor_ref), custom_call_target="tpu_custom_call" | custom-call | flops 805306368 | bytes 5242880 | tf_op jit(solution)/shard_map/fields_lanes/pallas_call | solution.py:496
  570.1 11.8 %fields_lanes.7.refs_2_ = f32[8,2,4,32,256]{4,3,2,1,0:T(8,128)} custom-call(f32[8,2,32,512]{3,2,1,0:T(8,128)} %copy-done, bf16[64,512,256]{2,1,0:T(8,128)(2,1)} %constant.71.clone.table_ref, f32[64,8,128]{2,1,0:T(8,128)} %constant.75.clone.factor_ref), custom_call_target="tpu_custom_call" | custom-call | flops 805306368 | bytes 5242880 | tf_op jit(solution)/shard_map/fields_lanes/pallas_call | solution.py:496
  581.9 11.8 %fields_lanes.8.refs_1_ = f32[8,2,4,32,256]{4,3,2,1,0:T(8,128)} custom-call(f32[8,2,32,512]{3,2,1,0:T(8,128)} %all-to-all-done.8.t_ref, bf16[64,512,256]{2,1,0:T(8,128)(2,1)} %constant.71.clone.table_ref, f32[64,8,128]{2,1,0:T(8,128)} %constant.75.clone.factor_ref), custom_call_target="tpu_custom_call" | custom-call | flops 805306368 | bytes 5242880 | tf_op jit(solution)/shard_map/fields_lanes/pallas_call | solution.py:496
  593.6 4.1 all-to-all-start.9
  597.8 2.7 fusion.4.refs_5_
  600.5 7.0 %all-to-all-done.9.t_ref = f32[8,1,32,512]{3,2,1,0:T(8,128)S(1)} async-done(((f32[8,1,32,512]{3,2,1,0:T(8,128)}), f32[8,1,32,512]{3,2,1,0:T(8,128)S(1)}, u32[]{:S(2)}, u32[]{:S(2)}) %all-to-all-start.9) | async-done | bytes 524320 | tf_op jit(solution)/shard_map/all_to_all | solution.py:640
  607.5 0.8 copy-done.1
  608.3 6.5 %fields_lanes.9.refs_0_ = f32[8,1,4,32,256]{4,3,2,1,0:T(8,128)} custom-call(f32[8,1,32,512]{3,2,1,0:T(8,128)} %copy-done.1, bf16[64,512,256]{2,1,0:T(8,128)(2,1)} %constant.71.clone.table_ref, f32[64,8,128]{2,1,0:T(8,128)} %constant.75.clone.factor_ref), custom_call_target="tpu_custom_call" | custom-call | flops 402653184 | bytes 2621440 | tf_op jit(solution)/shard_map/fields_lanes/pallas_call | solution.py:496
  614.8 17.2 %ray_step.1 = f32[6,32,16384]{2,1,0:T(8,128)} custom-call(f32[1]{0:T(128)S(6)} %copy.29.weight_ref, f32[8,1,4,32,256]{4,3,2,1,0:T(8,128)} %fields_lanes.9.refs_0_, f32[8,2,4,32,256]{4,3,2,1,0:T(8,128)} %fields_lanes.8.refs_1_, f32[8,2,4,32,256]{4,3,2,1,0:T(8,128)} %fields_lanes.7.refs_2_, f32[8,2,4,32,256]{4,3,2,1,0:T(8,128)} %fields_lanes.6.refs_3_, ...), custom_call_target="tpu_custom_call" | custom-call | flops 52428800 | bytes 37748736 | tf_op jit(solution)/shard_map/ray_step/pallas_call | solution.py:563
  (28 shorter events, 0.5 us)
Async XLA Ops:
  43.6 5.4 copy-start.2
  43.6 54.8 %all-to-all-start = ((f32[8,1,512,256]{3,2,1,0:T(8,128)}), f32[8,1,512,256]{3,2,1,0:T(8,128)}, u32[]{:S(2)}, u32[]{:S(2)}) async-start(f32[8,1,512,256]{3,2,1,0:T(8,128)} %column_lanes.5), calls=%async_computation | async-start | bytes 8388608 | tf_op jit(solution)/shard_map/all_to_all | solution.py:640
  48.9 408.6 %all-reduce.2.cloned.1.call-start = ((), (), s32[]{:S(2)}) async-start(), calls=%async_computation.15 | async-start | bytes 262144 | tf_op jit(solution)/shard_map/psum | solution.py:591
  53.8 0.5 copy-start.3
  98.4 99.4 %all-to-all-start.4 = ((f32[8,2,512,256]{3,2,1,0:T(8,128)}), f32[8,2,512,256]{3,2,1,0:T(8,128)}, u32[]{:S(2)}, u32[]{:S(2)}) async-start(f32[8,2,512,256]{3,2,1,0:T(8,128)} %column_lanes.8), calls=%async_computation.6 | async-start | bytes 16777216 | tf_op jit(solution)/shard_map/all_to_all | solution.py:640
  103.4 389.0 %reduce-scatter.8.cloned.1.call-start = ((), (), s32[]{:S(2)}) async-start(), calls=%async_computation.17 | async-start | bytes 2621440 | tf_op jit(solution)/shard_map/reduce_scatter | solution.py:660
  197.8 99.3 %all-to-all-start.1 = ((f32[8,2,512,256]{3,2,1,0:T(8,128)}), f32[8,2,512,256]{3,2,1,0:T(8,128)}, u32[]{:S(2)}, u32[]{:S(2)}) async-start(f32[8,2,512,256]{3,2,1,0:T(8,128)} %column_lanes.6), calls=%async_computation.1 | async-start | bytes 16777216 | tf_op jit(solution)/shard_map/all_to_all | solution.py:640
  202.7 303.5 %reduce-scatter.10.cloned.1.call-start = ((), (), s32[]{:S(2)}) async-start(), calls=%async_computation.18 | async-start | bytes 5242880 | tf_op jit(solution)/shard_map/reduce_scatter | solution.py:660
  297.1 99.0 %all-to-all-start.7 = ((f32[8,2,512,256]{3,2,1,0:T(8,128)}), f32[8,2,512,256]{3,2,1,0:T(8,128)}, u32[]{:S(2)}, u32[]{:S(2)}) async-start(f32[8,2,512,256]{3,2,1,0:T(8,128)} %column_lanes.9), calls=%async_computation.11 | async-start | bytes 16777216 | tf_op jit(solution)/shard_map/all_to_all | solution.py:640
  302.0 224.1 %reduce-scatter.12.cloned.1.call-start = ((), (), s32[]{:S(2)}) async-start(), calls=%async_computation.19 | async-start | bytes 5242880 | tf_op jit(solution)/shard_map/reduce_scatter | solution.py:660
  396.1 62.4 %all-to-all-start.2 = ((f32[8,1,512,256]{3,2,1,0:T(8,128)}), f32[8,1,512,256]{3,2,1,0:T(8,128)}, u32[]{:S(2)}, u32[]{:S(2)}) async-start(f32[8,1,512,256]{3,2,1,0:T(8,128)} %column_lanes.7), calls=%async_computation.2 | async-start | bytes 8388608 | tf_op jit(solution)/shard_map/all_to_all | solution.py:640
  400.6 144.4 %reduce-scatter.14.cloned.1.call-start = ((), (), s32[]{:S(2)}) async-start(), calls=%async_computation.20 | async-start | bytes 5242880 | tf_op jit(solution)/shard_map/reduce_scatter | solution.py:660
  457.4 136.2 %reduce-scatter.6.cloned.1.call-start = ((), (), s32[]{:S(2)}) async-start(), calls=%async_computation.16 | async-start | bytes 2621440 | tf_op jit(solution)/shard_map/reduce_scatter | solution.py:660
  526.1 18.9 %all-to-all-start.6 = ((f32[8,2,32,512]{3,2,1,0:T(8,128)}), f32[8,2,32,512]{3,2,1,0:T(8,128)S(1)}, u32[]{:S(2)}, u32[]{:S(2)}) async-start(f32[8,2,32,512]{3,2,1,0:T(8,128)} %bitcast.34), calls=%async_computation.10 | async-start | bytes 2097152 | tf_op jit(solution)/shard_map/all_to_all | solution.py:640
  545.0 10.8 %copy-start = (f32[8,2,32,512]{3,2,1,0:T(8,128)}, f32[8,2,32,512]{3,2,1,0:T(8,128)S(1)}, u32[]{:S(2)}) copy-start(f32[8,2,32,512]{3,2,1,0:T(8,128)S(1)} %all-to-all-done.6.t_ref) | copy-start | bytes 3145732
  545.0 36.9 %all-to-all-start.8 = ((f32[8,2,32,512]{3,2,1,0:T(8,128)}), f32[8,2,32,512]{3,2,1,0:T(8,128)}, u32[]{:S(2)}, u32[]{:S(2)}) async-start(f32[8,2,32,512]{3,2,1,0:T(8,128)} %bitcast.33), calls=%async_computation.13 | async-start | bytes 2097152 | tf_op jit(solution)/shard_map/all_to_all | solution.py:640
  593.6 13.9 %all-to-all-start.9 = ((f32[8,1,32,512]{3,2,1,0:T(8,128)}), f32[8,1,32,512]{3,2,1,0:T(8,128)S(1)}, u32[]{:S(2)}, u32[]{:S(2)}) async-start(f32[8,1,32,512]{3,2,1,0:T(8,128)} %bitcast.38), calls=%async_computation.14 | async-start | bytes 1048576 | tf_op jit(solution)/shard_map/all_to_all | solution.py:640
  607.5 0.8 copy-start.1
Sparse Core Ops, SparseCore 0:
  55.3 182.9 all-reduce.1
Sparse Core Ops, SparseCore 1:
  151.5 45.9 reduce-scatter.7
  275.1 79.0 reduce-scatter.9
  367.5 78.7 reduce-scatter.11
  457.5 79.0 reduce-scatter.13
  538.9 43.9 reduce-scatter.5

commit v2 on v1

--- a/solution.py
+++ b/solution.py
@@ -250,34 +250,32 @@
 
 
 def lanes_kernel(y_ref, table_ref, out_ref):
-    own = y_ref.shape[2] // STRIDE
-    sides = []
-    for side in range(2):
-        pieces = [y_ref[0, side, pl.ds(s, own, stride=STRIDE), :] for s in range(STRIDE)]
-        whole = jnp.concatenate(pieces, axis=0)
-        sides.append(whole)
-    high, low = split(jnp.concatenate(sides, axis=1))
-    table = table_ref[0]
-    top, rest = table[: 2 * LANES], table[2 * LANES :]
-    out_ref[0, 0] = dot(
-        jnp.concatenate([high, high, low], axis=1), jnp.concatenate([top, rest, top], axis=0)
-    )
-
-
-def over_lanes(grouped, table, devices, begin, count):
-    slots, _, rows, lanes = grouped.shape
+    own = y_ref.shape[3] // STRIDE
+    for d in range(y_ref.shape[0]):
+        sides = []
+        for side in range(2):
+            pieces = [y_ref[d, 0, side, pl.ds(s, own, stride=STRIDE), :] for s in range(STRIDE)]
+            sides.append(jnp.concatenate(pieces, axis=0))
+        high, low = split(jnp.concatenate(sides, axis=1))
+        table = table_ref[d, 0]
+        top, rest = table[: 2 * LANES], table[2 * LANES :]
+        out_ref[d, 0] = dot(
+            jnp.concatenate([high, high, low], axis=1), jnp.concatenate([top, rest, top], axis=0)
+        )
+
+
+def over_lanes(grouped, table, begin, count):
+    devices, owned, _, rows, lanes = grouped.shape
     width = 2 * lanes
-    owned = slots // devices
+    step = math.gcd(devices, 2)
     return pl.pallas_call(
         lanes_kernel,
-        grid=(devices, count),
+        grid=(devices // step, count),
         in_specs=[
-            pl.BlockSpec(
-                (1, 2, rows, lanes), lambda d, i: (d * owned + begin + i, 0, 0, 0)
-            ),
-            pl.BlockSpec((1, 2 * width, width), lambda d, i: (d * owned + begin + i, 0, 0)),
+            pl.BlockSpec((step, 1, 2, rows, lanes), lambda d, i: (d, begin + i, 0, 0, 0)),
+            pl.BlockSpec((step, 1, 2 * width, width), lambda d, i: (d, begin + i, 0, 0)),
         ],
-        out_specs=pl.BlockSpec((1, 1, rows, width), lambda d, i: (d, i, 0, 0)),
+        out_specs=pl.BlockSpec((step, 1, rows, width), lambda d, i: (d, i, 0, 0)),
         out_shape=jax.ShapeDtypeStruct((devices, count, rows, width), F32),
         compiler_params=params(),
         cost_estimate=pl.CostEstimate(
@@ -458,20 +456,24 @@
 
 
 def back_kernel(t_ref, table_ref, factor_ref, out_ref):
-    t = t_ref[0, 0]
-    t0r, t0i, t1r, t1i = (t[:, n * LANES : (n + 1) * LANES] for n in range(4))
-    factor = factor_ref[0]
-    by_r, by_c, by_cc, by_rc = (factor[n : n + 1] for n in range(4))
-    real = jnp.concatenate([-t1i * by_r, -t0i * by_c, t0r * by_cc, t1r * by_rc], axis=0)
-    imaginary = jnp.concatenate([t1r * by_r, t0r * by_c, t0i * by_cc, t1i * by_rc], axis=0)
-    high, low = split(jnp.concatenate([real, imaginary], axis=1))
-    table = table_ref[0]
-    top, rest = table[: 2 * LANES], table[2 * LANES :]
     form = (((1,), (1,)), ((), ()))
-    total = lax.dot_general(high, top, form, preferred_element_type=F32)
-    total += lax.dot_general(high, rest, form, preferred_element_type=F32)
-    total += lax.dot_general(low, top, form, preferred_element_type=F32)
-    out_ref[0, 0] = total.reshape(out_ref.shape[2:])
+    for d in range(t_ref.shape[0]):
+        t = t_ref[d, 0]
+        t0r, t0i, t1r, t1i = (t[:, n * LANES : (n + 1) * LANES] for n in range(4))
+        factor = factor_ref[d, 0]
+        by_r, by_c, by_cc, by_rc = (factor[n : n + 1] for n in range(4))
+        real = jnp.concatenate([-t1i * by_r, -t0i * by_c, t0r * by_cc, t1r * by_rc], axis=0)
+        imaginary = jnp.concatenate([t1r * by_r, t0r * by_c, t0i * by_cc, t1i * by_rc], axis=0)
+        high, low = split(jnp.concatenate([real, imaginary], axis=1))
+        table = table_ref[d, 0]
+        top, rest = table[: 2 * LANES], table[2 * LANES :]
+        total = lax.dot_general(
+            jnp.concatenate([high, high, low], axis=1),
+            jnp.concatenate([top, rest, top], axis=1),
+            form,
+            preferred_element_type=F32,
+        )
+        out_ref[d, 0] = total.reshape(out_ref.shape[2:])
 
 
 def field_factors(length):
@@ -491,17 +493,16 @@
 
 def back_over_lanes(returned, table, factors, begin):
     devices, count, own, width = returned.shape
-    owned = table.shape[0] // devices
-    slot = lambda d, i: (d * owned + begin + i, 0, 0)
+    step = math.gcd(devices, 4)
     return pl.pallas_call(
         back_kernel,
-        grid=(devices, count),
+        grid=(devices // step, count),
         in_specs=[
-            pl.BlockSpec((1, 1, own, width), lambda d, i: (d, i, 0, 0)),
-            pl.BlockSpec((1,) + table.shape[1:], slot),
-            pl.BlockSpec((1,) + factors.shape[1:], slot),
+            pl.BlockSpec((step, 1, own, width), lambda d, i: (d, i, 0, 0)),
+            pl.BlockSpec((step, 1) + table.shape[2:], lambda d, i: (d, begin + i, 0, 0)),
+            pl.BlockSpec((step, 1) + factors.shape[2:], lambda d, i: (d, begin + i, 0, 0)),
         ],
-        out_specs=pl.BlockSpec((1, 1, 4, own, 2 * LANES), lambda d, i: (d, i, 0, 0, 0)),
+        out_specs=pl.BlockSpec((step, 1, 4, own, 2 * LANES), lambda d, i: (d, i, 0, 0, 0)),
         out_shape=jax.ShapeDtypeStruct((devices, count, 4, own, 2 * LANES), F32),
         compiler_params=params(),
         cost_estimate=pl.CostEstimate(
@@ -624,29 +625,28 @@
     runs = parted(owned)
     pieces = len(runs)
     field = convergence[0]
-    table = jnp.asarray(column_table(length))
+    table = jnp.asarray(column_table(length).reshape(devices, owned, 4 * LANES, 2 * LANES))
     tables = [jnp.asarray(t) for t in ray_tables(length // STRIDE, own * devices, length)]
-    factors = jnp.asarray(field_factors(length))
+    factors = jnp.asarray(field_factors(length).reshape(devices, owned, TILE, LANES))
     grouped, sums = over_groups(field)
+    grouped = grouped.reshape(devices, owned, *grouped.shape[1:])
     totals = column_totals(sums)
     place = jnp.stack([lax.axis_index("row"), lax.axis_index("col") * owned]).astype(jnp.int32)
 
     def send(step, *after):
         begin, count = runs[step]
         held = lax.optimization_barrier((grouped, *after))[0]
-        return over_lanes(held, table, devices, begin, count)
+        return over_lanes(held, table, begin, count)
 
     def exchange(value):
         return lax.all_to_all(value, "col", split_axis=0, concat_axis=0, tiled=True)
 
     sent = {step: send(step) for step in range(min(2, pieces))}
-    arrived = {}
-    for step in range(pieces):
+    arrived, partial, summed = {}, {}, {}
+    for step, (begin, count) in enumerate(runs):
         arrived[step] = exchange(sent[step])
         if step + 2 < pieces:
             sent[step + 2] = send(step + 2, arrived[step])
-    summed = {}
-    for step, (begin, count) in enumerate(runs):
         held = arrived[step]
         if step + 2 < pieces:
             held = lax.optimization_barrier((held, sent[step + 2]))[0]
@@ -656,8 +656,10 @@
         if begin == 0:
             late = lax.optimization_barrier((totals, arrived[step]))[0]
             mean = jnp.mean(late[0]).reshape(1)
-        partial = to_rays(place + shift, mean, held, tables, planes)
-        summed[step] = lax.psum_scatter(partial, "row", scatter_dimension=0, tiled=True)[0]
+        partial[step] = to_rays(place + shift, mean, held, tables, planes)
+        summed[step] = lax.psum_scatter(
+            partial[step], "row", scatter_dimension=0, tiled=True
+        )[0]
     done = {}
     for step, (begin, _) in enumerate(runs):
         held = summed[step]

time: 644 us -> 626 us (0.972)
  Pallas kernels: 392 us -> 356 us
  waiting for transfers between devices: 141 us -> 162 us
    pallas_call x10, Pallas kernels: 112 us -> 75.9 us  [the longest x5 51.7 us: over_lanes(): pl.pallas_call(lanes_kernel, grid=(devices // step, count), in_specs=[pl....]
    all_to_all x8, waiting for transfers between devices: 141 us -> 152 us  [exchange(): return lax.all_to_all(value, 'col', split_axis=0, concat_axis=0, tiled=True)]
    reduce_scatter x5, waiting for transfers between devices: 0.03 us -> 10.1 us  [body(): lax.psum_scatter(partial[step], 'row', scatter_dimension=0, tiled=True)[0]]
  transfers between devices with their start and end apart: 14 -> 14, of which waited for: 6 -> 7; matrix products, arithmetic and copies ran while one was open for 3% -> 3% of each run, Pallas kernels for 52% -> 48%
where the time goes in v2:
time: 626 us; the launch traced here: 624 us
  Pallas kernels  356 us (57%)
  waiting for transfers between devices  162 us (26%)
  starting transfers between devices  37.1 us (6%)
  blocking collectives  33.5 us (5%)
  between operations  17.1 us (3%)
  local copies, waits for them, and re-layouts  9.86 us (2%)
  other arithmetic  8.62 us (1%)
    pallas_call x5, Pallas kernels, to_rays(): pl.pallas_call(functools.partial(rays_kernel, mean is not None), grid_spe...  235 us
    all_to_all x8, waiting for transfers between devices, exchange(): return lax.all_to_all(value, 'col', split_axis=0, concat_axis=0, tiled=True)  152 us
    pallas_call x5, Pallas kernels, over_lanes(): pl.pallas_call(lanes_kernel, grid=(devices // step, count), in_specs=[pl....  51.7 us
    all_to_all x8, starting transfers between devices, exchange(): return lax.all_to_all(value, 'col', split_axis=0, concat_axis=0, tiled=True)  36.5 us
    all_to_all x2, blocking collectives, exchange(): return lax.all_to_all(value, 'col', split_axis=0, concat_axis=0, tiled=True)  33.5 us
    pallas_call x1, Pallas kernels, over_groups(): pl.pallas_call(groups_kernel, grid=(rows // step,), in_specs=[pl.BlockSpe...  27.8 us
    pallas_call x5, Pallas kernels, back_over_lanes(): pl.pallas_call(back_kernel, grid=(devices // step, count), in_specs=[pl.B...  24.2 us
    pallas_call x1, Pallas kernels, advance(): pl.pallas_call(advance_kernel, grid=(own // TILE,), in_specs=[pl.BlockSpe...  17.2 us
  transfers between devices with their start and end apart: 14, of which 7 were waited for; matrix products, arithmetic and copies ran while one was open for 3% of the time, Pallas kernels for 48%

profile of v2, /device:TPU:0, one launch (start us, length us, event | category | flops | bytes accessed | tf_op | source)
XLA Modules:
  0.0 623.8 jit_solution(15996385270542510308)
XLA Ops:
  7.4 27.8 %column_groups.1 = (f32[64,2,512,128]{3,2,1,0:T(8,128)}, f32[8,16384]{1,0:T(8,128)}) custom-call(bf16[512,16384]{1,0:T(8,128)(2,1)} %bitcast.34), custom_call_target="tpu_custom_call" | custom-call | flops 167772160 | bytes 50331648 | tf_op jit(solution)/shard_map/column_groups/pallas_call | solution.py:232
  35.2 7.0 %column_lanes.5 = f32[8,1,512,256]{3,2,1,0:T(8,128)} custom-call(f32[8,8,2,512,128]{4,3,2,1,0:T(8,128)} %bitcast.29, bf16[8,8,512,256]{3,2,1,0:T(8,128)(2,1)} %constant.71.clone.table_ref), custom_call_target="tpu_custom_call" | custom-call | flops 1610612736 | bytes 8388608 | tf_op jit(solution)/shard_map/column_lanes/pallas_call | solution.py:271
  42.2 5.3 all-to-all-start
  47.6 1.6 slice.13
  49.1 1.6 slice.12
  51.0 0.8 pad_maximum_fusion
  51.8 0.6 iota_add_fusion
  52.5 0.5 copy-done.3
  52.9 0.6 multiply_add_fusion
  53.5 12.6 %column_lanes.8 = f32[8,2,512,256]{3,2,1,0:T(8,128)} custom-call(f32[8,8,2,512,128]{4,3,2,1,0:T(8,128)} %bitcast.30, bf16[8,8,512,256]{3,2,1,0:T(8,128)(2,1)} %constant.71.clone.table_ref), custom_call_target="tpu_custom_call" | custom-call | flops 3221225472 | bytes 16777216 | tf_op jit(solution)/shard_map/column_lanes/pallas_call | solution.py:271
  66.1 30.9 %all-to-all-done = f32[8,1,512,256]{3,2,1,0:T(8,128)} async-done(((f32[8,1,512,256]{3,2,1,0:T(8,128)}), f32[8,1,512,256]{3,2,1,0:T(8,128)}, u32[]{:S(2)}, u32[]{:S(2)}) %all-to-all-start) | async-done | bytes 4194336 | tf_op jit(solution)/shard_map/all_to_all | solution.py:642
  97.0 5.0 all-to-all-start.4
  102.0 12.6 %column_lanes.6 = f32[8,2,512,256]{3,2,1,0:T(8,128)} custom-call(f32[8,8,2,512,128]{4,3,2,1,0:T(8,128)} %bitcast.31, bf16[8,8,512,256]{3,2,1,0:T(8,128)(2,1)} %constant.71.clone.table_ref), custom_call_target="tpu_custom_call" | custom-call | flops 3221225472 | bytes 16777216 | tf_op jit(solution)/shard_map/column_lanes/pallas_call | solution.py:271
  114.6 32.4 %ray_rows.6 = f32[4,8,1,32,512]{4,3,2,1,0:T(8,128)} custom-call(s32[2]{0:T(128)} %get-tuple-element.31.place_ref, f32[1]{0:T(128)} %constant.64.clone.1.mean_ref, f32[8,1,16,32,256]{4,3,2,1,0:T(8,128)} %bitcast.10.x_ref, bf16[1040,768]{1,0:T(8,128)(2,1)} %constant.72.clone.forward_ref, f32[520,128]{1,0:T(8,128)} %constant.73.clone.twist_ref, ...), custom_call_target="tpu_custom_call" | custom-call | flops 78114717696 | bytes 6291456 | tf_op jit(solution)/shard_map/ray_rows/pallas_call | solution.py:420
  147.0 49.4 %all-to-all-done.4 = f32[8,2,512,256]{3,2,1,0:T(8,128)} async-done(((f32[8,2,512,256]{3,2,1,0:T(8,128)}), f32[8,2,512,256]{3,2,1,0:T(8,128)}, u32[]{:S(2)}, u32[]{:S(2)}) %all-to-all-start.4) | async-done | bytes 8388640 | tf_op jit(solution)/shard_map/all_to_all | solution.py:642
  196.4 5.0 all-to-all-start.1
  201.6 12.6 %column_lanes.9 = f32[8,2,512,256]{3,2,1,0:T(8,128)} custom-call(f32[8,8,2,512,128]{4,3,2,1,0:T(8,128)} %bitcast.32, bf16[8,8,512,256]{3,2,1,0:T(8,128)(2,1)} %constant.71.clone.table_ref), custom_call_target="tpu_custom_call" | custom-call | flops 3221225472 | bytes 16777216 | tf_op jit(solution)/shard_map/column_lanes/pallas_call | solution.py:271
  214.2 56.6 %ray_rows.7 = f32[4,8,2,32,512]{4,3,2,1,0:T(8,128)} custom-call(s32[2]{0:T(128)} %get-tuple-element.30.place_ref, f32[1]{0:T(128)} %constant.64.clone.1.mean_ref, f32[8,2,16,32,256]{4,3,2,1,0:T(8,128)} %bitcast.13.x_ref, bf16[1040,768]{1,0:T(8,128)(2,1)} %constant.72.clone.forward_ref, f32[520,128]{1,0:T(8,128)} %constant.73.clone.twist_ref, ...), custom_call_target="tpu_custom_call" | custom-call | flops 156229435392 | bytes 12582912 | tf_op jit(solution)/shard_map/ray_rows/pallas_call | solution.py:420
  270.9 24.7 %all-to-all-done.1 = f32[8,2,512,256]{3,2,1,0:T(8,128)} async-done(((f32[8,2,512,256]{3,2,1,0:T(8,128)}), f32[8,2,512,256]{3,2,1,0:T(8,128)}, u32[]{:S(2)}, u32[]{:S(2)}) %all-to-all-start.1) | async-done | bytes 8388640 | tf_op jit(solution)/shard_map/all_to_all | solution.py:642
  295.6 5.0 all-to-all-start.7
  300.6 7.0 %column_lanes.7 = f32[8,1,512,256]{3,2,1,0:T(8,128)} custom-call(f32[8,8,2,512,128]{4,3,2,1,0:T(8,128)} %bitcast.33, bf16[8,8,512,256]{3,2,1,0:T(8,128)(2,1)} %constant.71.clone.table_ref), custom_call_target="tpu_custom_call" | custom-call | flops 1610612736 | bytes 8388608 | tf_op jit(solution)/shard_map/column_lanes/pallas_call | solution.py:271
  307.6 56.7 %ray_rows.8 = f32[4,8,2,32,512]{4,3,2,1,0:T(8,128)} custom-call(s32[2]{0:T(128)} %get-tuple-element.29.place_ref, f32[1]{0:T(128)} %constant.64.clone.1.mean_ref, f32[8,2,16,32,256]{4,3,2,1,0:T(8,128)} %bitcast.15.x_ref, bf16[1040,768]{1,0:T(8,128)(2,1)} %constant.72.clone.forward_ref, f32[520,128]{1,0:T(8,128)} %constant.73.clone.twist_ref, ...), custom_call_target="tpu_custom_call" | custom-call | flops 156229435392 | bytes 12582912 | tf_op jit(solution)/shard_map/ray_rows/pallas_call | solution.py:420
  364.3 30.3 %all-to-all-done.7 = f32[8,2,512,256]{3,2,1,0:T(8,128)} async-done(((f32[8,2,512,256]{3,2,1,0:T(8,128)}), f32[8,2,512,256]{3,2,1,0:T(8,128)}, u32[]{:S(2)}, u32[]{:S(2)}) %all-to-all-start.7) | async-done | bytes 8388640 | tf_op jit(solution)/shard_map/all_to_all | solution.py:642
  394.6 4.6 all-to-all-start.2
  399.2 0.3 reduce-scatter.14.cloned.1.call-start
  399.4 56.7 %ray_rows.9 = f32[4,8,2,32,512]{4,3,2,1,0:T(8,128)} custom-call(s32[2]{0:T(128)} %get-tuple-element.25.place_ref, f32[1]{0:T(128)} %constant.64.clone.1.mean_ref, f32[8,2,16,32,256]{4,3,2,1,0:T(8,128)} %bitcast.17.x_ref, bf16[1040,768]{1,0:T(8,128)(2,1)} %constant.72.clone.forward_ref, f32[520,128]{1,0:T(8,128)} %constant.73.clone.twist_ref, ...), custom_call_target="tpu_custom_call" | custom-call | flops 156229435392 | bytes 12582912 | tf_op jit(solution)/shard_map/ray_rows/pallas_call | solution.py:420
  456.3 1.0 broadcast_multiply_fusion
  457.2 0.8 fusion.10
  458.6 32.4 %ray_rows.5 = f32[4,8,1,32,512]{4,3,2,1,0:T(8,128)} custom-call(s32[2]{0:T(128)} %copy-done.3, f32[1]{0:T(128)} %bitcast.6.mean_ref, f32[8,1,16,32,256]{4,3,2,1,0:T(8,128)} %bitcast.7.x_ref, bf16[1040,768]{1,0:T(8,128)(2,1)} %constant.72.clone.forward_ref, f32[520,128]{1,0:T(8,128)} %constant.73.clone.twist_ref, bf16[1024,2048]{1,0:T(8,128)(2,1)} %constant.74.clone.backward_ref), custom_call_target="tpu_custom_call" | custom-call | flops 78114717696 | bytes 6291456 | tf_op jit(solution)/shard_map/ray_rows/pallas_call | solution.py:420
  491.1 13.9 %all_to_all.50.t_ref = f32[8,1,32,512]{3,2,1,0:T(8,128)} all-to-all(f32[8,1,32,512]{3,2,1,0:T(8,128)} %bitcast.43), channel_id=1, replica_groups=mesh['shell'=1,'row'=4,'col'=8] {'col'}, dimensions={0} | all-to-all | bytes 1048576 | tf_op jit(solution)/shard_map/all_to_all | solution.py:642
  505.0 19.6 %all_to_all.51.t_ref = f32[8,2,32,512]{3,2,1,0:T(8,128)} all-to-all(f32[8,2,32,512]{3,2,1,0:T(8,128)} %bitcast.38), channel_id=1, replica_groups=mesh['shell'=1,'row'=4,'col'=8] {'col'}, dimensions={0} | all-to-all | bytes 2097152 | tf_op jit(solution)/shard_map/all_to_all | solution.py:642
  524.6 3.6 all-to-all-start.6
  528.9 5.5 slice.16
  534.3 9.2 %all-to-all-done.6.t_ref = f32[8,2,32,512]{3,2,1,0:T(8,128)S(1)} async-done(((f32[8,2,32,512]{3,2,1,0:T(8,128)}), f32[8,2,32,512]{3,2,1,0:T(8,128)S(1)}, u32[]{:S(2)}, u32[]{:S(2)}) %all-to-all-start.6) | async-done | bytes 1048608 | tf_op jit(solution)/shard_map/all_to_all | solution.py:642
  543.5 4.5 all-to-all-start.8
  548.1 3.5 fields_lanes.5.refs_4_
  551.6 0.6 multiply_reduce_fusion
  552.8 1.2 fusion
  554.1 5.8 fields_lanes.6.refs_3_
  559.9 5.7 fields_lanes.7.refs_2_
  565.6 5.8 fields_lanes.8.refs_1_
  571.3 10.0 %reduce-scatter.6.cloned.1.call-done = f32[1,8,1,32,512]{4,3,1,2,0:T(8,128)} async-done(((f32[4,8,1,32,512]{4,3,1,2,0:T(8,128)}), f32[1,8,1,32,512]{4,3,1,2,0:T(8,128)}) %reduce-scatter.6.cloned.1.call-update) | async-done | bytes 524304 | tf_op jit(solution)/shard_map/reduce_scatter | solution.py:660
  581.4 3.6 all-to-all-start.9
  585.0 2.7 fusion.4.refs_5_
  587.7 7.0 %all-to-all-done.9.t_ref = f32[8,1,32,512]{3,2,1,0:T(8,128)S(1)} async-done(((f32[8,1,32,512]{3,2,1,0:T(8,128)}), f32[8,1,32,512]{3,2,1,0:T(8,128)S(1)}, u32[]{:S(2)}, u32[]{:S(2)}) %all-to-all-start.9) | async-done | bytes 524320 | tf_op jit(solution)/shard_map/all_to_all | solution.py:642
  594.7 0.8 copy-done.1
  595.5 3.4 fields_lanes.9.refs_0_
  598.9 17.2 %ray_step.1 = f32[6,32,16384]{2,1,0:T(8,128)} custom-call(f32[1]{0:T(128)S(6)} %copy.29.weight_ref, f32[8,1,4,32,256]{4,3,2,1,0:T(8,128)} %fields_lanes.9.refs_0_, f32[8,2,4,32,256]{4,3,2,1,0:T(8,128)} %fields_lanes.8.refs_1_, f32[8,2,4,32,256]{4,3,2,1,0:T(8,128)} %fields_lanes.7.refs_2_, f32[8,2,4,32,256]{4,3,2,1,0:T(8,128)} %fields_lanes.6.refs_3_, ...), custom_call_target="tpu_custom_call" | custom-call | flops 52428800 | bytes 37748736 | tf_op jit(solution)/shard_map/ray_step/pallas_call | solution.py:564
  (28 shorter events, 0.9 us)
Async XLA Ops:
  42.2 5.4 copy-start.2
  42.2 54.8 %all-to-all-start = ((f32[8,1,512,256]{3,2,1,0:T(8,128)}), f32[8,1,512,256]{3,2,1,0:T(8,128)}, u32[]{:S(2)}, u32[]{:S(2)}) async-start(f32[8,1,512,256]{3,2,1,0:T(8,128)} %column_lanes.5), calls=%async_computation | async-start | bytes 8388608 | tf_op jit(solution)/shard_map/all_to_all | solution.py:642
  47.5 408.7 %all-reduce.2.cloned.1.call-start = ((), (), s32[]{:S(2)}) async-start(), calls=%async_computation.15 | async-start | bytes 262144 | tf_op jit(solution)/shard_map/psum | solution.py:592
  52.5 0.5 copy-start.3
  97.0 99.4 %all-to-all-start.4 = ((f32[8,2,512,256]{3,2,1,0:T(8,128)}), f32[8,2,512,256]{3,2,1,0:T(8,128)}, u32[]{:S(2)}, u32[]{:S(2)}) async-start(f32[8,2,512,256]{3,2,1,0:T(8,128)} %column_lanes.8), calls=%async_computation.6 | async-start | bytes 16777216 | tf_op jit(solution)/shard_map/all_to_all | solution.py:642
  102.0 389.2 %reduce-scatter.8.cloned.1.call-start = ((), (), s32[]{:S(2)}) async-start(), calls=%async_computation.17 | async-start | bytes 2621440 | tf_op jit(solution)/shard_map/reduce_scatter | solution.py:660
  196.4 99.2 %all-to-all-start.1 = ((f32[8,2,512,256]{3,2,1,0:T(8,128)}), f32[8,2,512,256]{3,2,1,0:T(8,128)}, u32[]{:S(2)}, u32[]{:S(2)}) async-start(f32[8,2,512,256]{3,2,1,0:T(8,128)} %column_lanes.6), calls=%async_computation.1 | async-start | bytes 16777216 | tf_op jit(solution)/shard_map/all_to_all | solution.py:642
  201.4 303.7 %reduce-scatter.10.cloned.1.call-start = ((), (), s32[]{:S(2)}) async-start(), calls=%async_computation.18 | async-start | bytes 5242880 | tf_op jit(solution)/shard_map/reduce_scatter | solution.py:660
  295.6 99.0 %all-to-all-start.7 = ((f32[8,2,512,256]{3,2,1,0:T(8,128)}), f32[8,2,512,256]{3,2,1,0:T(8,128)}, u32[]{:S(2)}, u32[]{:S(2)}) async-start(f32[8,2,512,256]{3,2,1,0:T(8,128)} %column_lanes.9), calls=%async_computation.11 | async-start | bytes 16777216 | tf_op jit(solution)/shard_map/all_to_all | solution.py:642
  300.5 224.1 %reduce-scatter.12.cloned.1.call-start = ((), (), s32[]{:S(2)}) async-start(), calls=%async_computation.19 | async-start | bytes 5242880 | tf_op jit(solution)/shard_map/reduce_scatter | solution.py:660
  394.6 62.6 %all-to-all-start.2 = ((f32[8,1,512,256]{3,2,1,0:T(8,128)}), f32[8,1,512,256]{3,2,1,0:T(8,128)}, u32[]{:S(2)}, u32[]{:S(2)}) async-start(f32[8,1,512,256]{3,2,1,0:T(8,128)} %column_lanes.7), calls=%async_computation.2 | async-start | bytes 8388608 | tf_op jit(solution)/shard_map/all_to_all | solution.py:642
  399.2 144.4 %reduce-scatter.14.cloned.1.call-start = ((), (), s32[]{:S(2)}) async-start(), calls=%async_computation.20 | async-start | bytes 5242880 | tf_op jit(solution)/shard_map/reduce_scatter | solution.py:660
  456.2 125.2 %reduce-scatter.6.cloned.1.call-start = ((), (), s32[]{:S(2)}) async-start(), calls=%async_computation.16 | async-start | bytes 2621440 | tf_op jit(solution)/shard_map/reduce_scatter | solution.py:660
  524.6 18.9 %all-to-all-start.6 = ((f32[8,2,32,512]{3,2,1,0:T(8,128)}), f32[8,2,32,512]{3,2,1,0:T(8,128)S(1)}, u32[]{:S(2)}, u32[]{:S(2)}) async-start(f32[8,2,32,512]{3,2,1,0:T(8,128)} %bitcast.40), calls=%async_computation.10 | async-start | bytes 2097152 | tf_op jit(solution)/shard_map/all_to_all | solution.py:642
  543.5 8.0 %copy-start = (f32[8,2,32,512]{3,2,1,0:T(8,128)}, f32[8,2,32,512]{3,2,1,0:T(8,128)S(1)}, u32[]{:S(2)}) copy-start(f32[8,2,32,512]{3,2,1,0:T(8,128)S(1)} %all-to-all-done.6.t_ref) | copy-start | bytes 3145732
  543.5 22.0 %all-to-all-start.8 = ((f32[8,2,32,512]{3,2,1,0:T(8,128)}), f32[8,2,32,512]{3,2,1,0:T(8,128)}, u32[]{:S(2)}, u32[]{:S(2)}) async-start(f32[8,2,32,512]{3,2,1,0:T(8,128)} %bitcast.39), calls=%async_computation.13 | async-start | bytes 2097152 | tf_op jit(solution)/shard_map/all_to_all | solution.py:642
  581.4 13.4 %all-to-all-start.9 = ((f32[8,1,32,512]{3,2,1,0:T(8,128)}), f32[8,1,32,512]{3,2,1,0:T(8,128)S(1)}, u32[]{:S(2)}, u32[]{:S(2)}) async-start(f32[8,1,32,512]{3,2,1,0:T(8,128)} %bitcast.44), calls=%async_computation.14 | async-start | bytes 1048576 | tf_op jit(solution)/shard_map/all_to_all | solution.py:642
  594.7 0.8 copy-start.1
Sparse Core Ops, SparseCore 0:
  53.9 167.8 all-reduce.1
Sparse Core Ops, SparseCore 1:
  147.1 45.9 reduce-scatter.7
  270.9 78.9 reduce-scatter.9
  364.4 79.0 reduce-scatter.11
  456.3 78.8 reduce-scatter.13
  537.4 43.9 reduce-scatter.5

commit v3 on v2

--- a/solution.py
+++ b/solution.py
@@ -346,7 +346,6 @@
             else:
                 squared_safe = squared
             inverse = pl.reciprocal(squared_safe, approx=True)
-            inverse = inverse * (2.0 - squared_safe * inverse)
             inverse = inverse * (2.0 - squared_safe * inverse)
             if a == 0:
                 inverse = jnp.where(squared > 0.0, inverse, 0.0)
@@ -493,7 +492,7 @@
 
 def back_over_lanes(returned, table, factors, begin):
     devices, count, own, width = returned.shape
-    step = math.gcd(devices, 4)
+    step = math.gcd(devices, 8)
     return pl.pallas_call(
         back_kernel,
         grid=(devices // step, count),

time: 626 us -> 626 us (level)
  transfers between devices with their start and end apart: 14 -> 14, of which waited for: 7 -> 7; matrix products, arithmetic and copies ran while one was open for 3% -> 3% of each run, Pallas kernels for 48% -> 47%
where the time goes in v3:
time: 626 us; the launch traced here: 623 us
  Pallas kernels  352 us (56%)
  waiting for transfers between devices  165 us (26%)
  starting transfers between devices  37.1 us (6%)
  blocking collectives  33.5 us (5%)
  between operations  17.1 us (3%)
  local copies, waits for them, and re-layouts  9.86 us (2%)
  other arithmetic  8.62 us (1%)
    pallas_call x5, Pallas kernels, to_rays(): pl.pallas_call(functools.partial(rays_kernel, mean is not None), grid_spe...  232 us
    all_to_all x8, waiting for transfers between devices, exchange(): return lax.all_to_all(value, 'col', split_axis=0, concat_axis=0, tiled=True)  154 us
    pallas_call x5, Pallas kernels, over_lanes(): pl.pallas_call(lanes_kernel, grid=(devices // step, count), in_specs=[pl....  51.7 us
    all_to_all x8, starting transfers between devices, exchange(): return lax.all_to_all(value, 'col', split_axis=0, concat_axis=0, tiled=True)  36.5 us
    all_to_all x2, blocking collectives, exchange(): return lax.all_to_all(value, 'col', split_axis=0, concat_axis=0, tiled=True)  33.5 us
    pallas_call x1, Pallas kernels, over_groups(): pl.pallas_call(groups_kernel, grid=(rows // step,), in_specs=[pl.BlockSpe...  27.8 us
    pallas_call x5, Pallas kernels, back_over_lanes(): pl.pallas_call(back_kernel, grid=(devices // step, count), in_specs=[pl.B...  23.2 us
    pallas_call x1, Pallas kernels, advance(): pl.pallas_call(advance_kernel, grid=(own // TILE,), in_specs=[pl.BlockSpe...  17.2 us
  transfers between devices with their start and end apart: 14, of which 7 were waited for; matrix products, arithmetic and copies ran while one was open for 3% of the time, Pallas kernels for 47%

profile of v3, /device:TPU:0, one launch (start us, length us, event | category | flops | bytes accessed | tf_op | source)
XLA Modules:
  0.0 623.3 jit_solution(8055622675496362737)
XLA Ops:
  7.4 27.8 %column_groups.1 = (f32[64,2,512,128]{3,2,1,0:T(8,128)}, f32[8,16384]{1,0:T(8,128)}) custom-call(bf16[512,16384]{1,0:T(8,128)(2,1)} %bitcast.34), custom_call_target="tpu_custom_call" | custom-call | flops 167772160 | bytes 50331648 | tf_op jit(solution)/shard_map/column_groups/pallas_call | solution.py:232
  35.2 7.0 %column_lanes.5 = f32[8,1,512,256]{3,2,1,0:T(8,128)} custom-call(f32[8,8,2,512,128]{4,3,2,1,0:T(8,128)} %bitcast.29, bf16[8,8,512,256]{3,2,1,0:T(8,128)(2,1)} %constant.71.clone.table_ref), custom_call_target="tpu_custom_call" | custom-call | flops 1610612736 | bytes 8388608 | tf_op jit(solution)/shard_map/column_lanes/pallas_call | solution.py:271
  42.2 5.3 all-to-all-start
  47.6 1.6 slice.13
  49.1 1.6 slice.12
  51.0 0.8 pad_maximum_fusion
  51.8 0.6 iota_add_fusion
  52.5 0.5 copy-done.3
  52.9 0.6 multiply_add_fusion
  53.5 12.6 %column_lanes.8 = f32[8,2,512,256]{3,2,1,0:T(8,128)} custom-call(f32[8,8,2,512,128]{4,3,2,1,0:T(8,128)} %bitcast.30, bf16[8,8,512,256]{3,2,1,0:T(8,128)(2,1)} %constant.71.clone.table_ref), custom_call_target="tpu_custom_call" | custom-call | flops 3221225472 | bytes 16777216 | tf_op jit(solution)/shard_map/column_lanes/pallas_call | solution.py:271
  66.1 30.9 %all-to-all-done = f32[8,1,512,256]{3,2,1,0:T(8,128)} async-done(((f32[8,1,512,256]{3,2,1,0:T(8,128)}), f32[8,1,512,256]{3,2,1,0:T(8,128)}, u32[]{:S(2)}, u32[]{:S(2)}) %all-to-all-start) | async-done | bytes 4194336 | tf_op jit(solution)/shard_map/all_to_all | solution.py:641
  97.0 5.0 all-to-all-start.4
  102.0 12.6 %column_lanes.6 = f32[8,2,512,256]{3,2,1,0:T(8,128)} custom-call(f32[8,8,2,512,128]{4,3,2,1,0:T(8,128)} %bitcast.31, bf16[8,8,512,256]{3,2,1,0:T(8,128)(2,1)} %constant.71.clone.table_ref), custom_call_target="tpu_custom_call" | custom-call | flops 3221225472 | bytes 16777216 | tf_op jit(solution)/shard_map/column_lanes/pallas_call | solution.py:271
  114.6 32.0 %ray_rows.6 = f32[4,8,1,32,512]{4,3,2,1,0:T(8,128)} custom-call(s32[2]{0:T(128)} %get-tuple-element.31.place_ref, f32[1]{0:T(128)} %constant.64.clone.1.mean_ref, f32[8,1,16,32,256]{4,3,2,1,0:T(8,128)} %bitcast.10.x_ref, bf16[1040,768]{1,0:T(8,128)(2,1)} %constant.72.clone.forward_ref, f32[520,128]{1,0:T(8,128)} %constant.73.clone.twist_ref, ...), custom_call_target="tpu_custom_call" | custom-call | flops 78114717696 | bytes 6291456 | tf_op jit(solution)/shard_map/ray_rows/pallas_call | solution.py:419
  146.6 49.8 %all-to-all-done.4 = f32[8,2,512,256]{3,2,1,0:T(8,128)} async-done(((f32[8,2,512,256]{3,2,1,0:T(8,128)}), f32[8,2,512,256]{3,2,1,0:T(8,128)}, u32[]{:S(2)}, u32[]{:S(2)}) %all-to-all-start.4) | async-done | bytes 8388640 | tf_op jit(solution)/shard_map/all_to_all | solution.py:641
  196.4 5.0 all-to-all-start.1
  201.6 12.6 %column_lanes.9 = f32[8,2,512,256]{3,2,1,0:T(8,128)} custom-call(f32[8,8,2,512,128]{4,3,2,1,0:T(8,128)} %bitcast.32, bf16[8,8,512,256]{3,2,1,0:T(8,128)(2,1)} %constant.71.clone.table_ref), custom_call_target="tpu_custom_call" | custom-call | flops 3221225472 | bytes 16777216 | tf_op jit(solution)/shard_map/column_lanes/pallas_call | solution.py:271
  214.2 55.8 %ray_rows.7 = f32[4,8,2,32,512]{4,3,2,1,0:T(8,128)} custom-call(s32[2]{0:T(128)} %get-tuple-element.30.place_ref, f32[1]{0:T(128)} %constant.64.clone.1.mean_ref, f32[8,2,16,32,256]{4,3,2,1,0:T(8,128)} %bitcast.13.x_ref, bf16[1040,768]{1,0:T(8,128)(2,1)} %constant.72.clone.forward_ref, f32[520,128]{1,0:T(8,128)} %constant.73.clone.twist_ref, ...), custom_call_target="tpu_custom_call" | custom-call | flops 156229435392 | bytes 12582912 | tf_op jit(solution)/shard_map/ray_rows/pallas_call | solution.py:419
  270.0 25.5 %all-to-all-done.1 = f32[8,2,512,256]{3,2,1,0:T(8,128)} async-done(((f32[8,2,512,256]{3,2,1,0:T(8,128)}), f32[8,2,512,256]{3,2,1,0:T(8,128)}, u32[]{:S(2)}, u32[]{:S(2)}) %all-to-all-start.1) | async-done | bytes 8388640 | tf_op jit(solution)/shard_map/all_to_all | solution.py:641
  295.6 5.0 all-to-all-start.7
  300.6 7.0 %column_lanes.7 = f32[8,1,512,256]{3,2,1,0:T(8,128)} custom-call(f32[8,8,2,512,128]{4,3,2,1,0:T(8,128)} %bitcast.33, bf16[8,8,512,256]{3,2,1,0:T(8,128)(2,1)} %constant.71.clone.table_ref), custom_call_target="tpu_custom_call" | custom-call | flops 1610612736 | bytes 8388608 | tf_op jit(solution)/shard_map/column_lanes/pallas_call | solution.py:271
  307.6 55.9 %ray_rows.8 = f32[4,8,2,32,512]{4,3,2,1,0:T(8,128)} custom-call(s32[2]{0:T(128)} %get-tuple-element.29.place_ref, f32[1]{0:T(128)} %constant.64.clone.1.mean_ref, f32[8,2,16,32,256]{4,3,2,1,0:T(8,128)} %bitcast.15.x_ref, bf16[1040,768]{1,0:T(8,128)(2,1)} %constant.72.clone.forward_ref, f32[520,128]{1,0:T(8,128)} %constant.73.clone.twist_ref, ...), custom_call_target="tpu_custom_call" | custom-call | flops 156229435392 | bytes 12582912 | tf_op jit(solution)/shard_map/ray_rows/pallas_call | solution.py:419
  363.5 31.1 %all-to-all-done.7 = f32[8,2,512,256]{3,2,1,0:T(8,128)} async-done(((f32[8,2,512,256]{3,2,1,0:T(8,128)}), f32[8,2,512,256]{3,2,1,0:T(8,128)}, u32[]{:S(2)}, u32[]{:S(2)}) %all-to-all-start.7) | async-done | bytes 8388640 | tf_op jit(solution)/shard_map/all_to_all | solution.py:641
  394.6 4.6 all-to-all-start.2
  399.2 0.3 reduce-scatter.14.cloned.1.call-start
  399.4 55.9 %ray_rows.9 = f32[4,8,2,32,512]{4,3,2,1,0:T(8,128)} custom-call(s32[2]{0:T(128)} %get-tuple-element.25.place_ref, f32[1]{0:T(128)} %constant.64.clone.1.mean_ref, f32[8,2,16,32,256]{4,3,2,1,0:T(8,128)} %bitcast.17.x_ref, bf16[1040,768]{1,0:T(8,128)(2,1)} %constant.72.clone.forward_ref, f32[520,128]{1,0:T(8,128)} %constant.73.clone.twist_ref, ...), custom_call_target="tpu_custom_call" | custom-call | flops 156229435392 | bytes 12582912 | tf_op jit(solution)/shard_map/ray_rows/pallas_call | solution.py:419
  455.4 1.0 broadcast_multiply_fusion
  456.4 0.8 fusion.10
  457.8 32.0 %ray_rows.5 = f32[4,8,1,32,512]{4,3,2,1,0:T(8,128)} custom-call(s32[2]{0:T(128)} %copy-done.3, f32[1]{0:T(128)} %bitcast.6.mean_ref, f32[8,1,16,32,256]{4,3,2,1,0:T(8,128)} %bitcast.7.x_ref, bf16[1040,768]{1,0:T(8,128)(2,1)} %constant.72.clone.forward_ref, f32[520,128]{1,0:T(8,128)} %constant.73.clone.twist_ref, bf16[1024,2048]{1,0:T(8,128)(2,1)} %constant.74.clone.backward_ref), custom_call_target="tpu_custom_call" | custom-call | flops 78114717696 | bytes 6291456 | tf_op jit(solution)/shard_map/ray_rows/pallas_call | solution.py:419
  489.9 13.9 %all_to_all.50.t_ref = f32[8,1,32,512]{3,2,1,0:T(8,128)} all-to-all(f32[8,1,32,512]{3,2,1,0:T(8,128)} %bitcast.43), channel_id=1, replica_groups=mesh['shell'=1,'row'=4,'col'=8] {'col'}, dimensions={0} | all-to-all | bytes 1048576 | tf_op jit(solution)/shard_map/all_to_all | solution.py:641
  503.8 19.6 %all_to_all.51.t_ref = f32[8,2,32,512]{3,2,1,0:T(8,128)} all-to-all(f32[8,2,32,512]{3,2,1,0:T(8,128)} %bitcast.38), channel_id=1, replica_groups=mesh['shell'=1,'row'=4,'col'=8] {'col'}, dimensions={0} | all-to-all | bytes 2097152 | tf_op jit(solution)/shard_map/all_to_all | solution.py:641
  523.4 3.6 all-to-all-start.6
  527.6 5.5 slice.16
  533.1 9.2 %all-to-all-done.6.t_ref = f32[8,2,32,512]{3,2,1,0:T(8,128)S(1)} async-done(((f32[8,2,32,512]{3,2,1,0:T(8,128)}), f32[8,2,32,512]{3,2,1,0:T(8,128)S(1)}, u32[]{:S(2)}, u32[]{:S(2)}) %all-to-all-start.6) | async-done | bytes 1048608 | tf_op jit(solution)/shard_map/all_to_all | solution.py:641
  542.3 4.5 all-to-all-start.8
  546.8 4.0 fields_lanes.5.refs_4_
  550.8 0.6 multiply_reduce_fusion
  552.1 1.2 fusion
  553.3 5.1 fields_lanes.6.refs_3_
  558.4 5.1 fields_lanes.7.refs_2_
  563.6 5.1 fields_lanes.8.refs_1_
  568.7 11.7 %reduce-scatter.6.cloned.1.call-done = f32[1,8,1,32,512]{4,3,1,2,0:T(8,128)} async-done(((f32[4,8,1,32,512]{4,3,1,2,0:T(8,128)}), f32[1,8,1,32,512]{4,3,1,2,0:T(8,128)}) %reduce-scatter.6.cloned.1.call-update) | async-done | bytes 524304 | tf_op jit(solution)/shard_map/reduce_scatter | solution.py:659
  580.4 3.6 all-to-all-start.9
  584.0 2.7 fusion.4.refs_5_
  586.8 7.0 %all-to-all-done.9.t_ref = f32[8,1,32,512]{3,2,1,0:T(8,128)S(1)} async-done(((f32[8,1,32,512]{3,2,1,0:T(8,128)}), f32[8,1,32,512]{3,2,1,0:T(8,128)S(1)}, u32[]{:S(2)}, u32[]{:S(2)}) %all-to-all-start.9) | async-done | bytes 524320 | tf_op jit(solution)/shard_map/all_to_all | solution.py:641
  593.8 0.8 copy-done.1
  594.6 3.9 fields_lanes.9.refs_0_
  598.5 17.2 %ray_step.1 = f32[6,32,16384]{2,1,0:T(8,128)} custom-call(f32[1]{0:T(128)S(6)} %copy.29.weight_ref, f32[8,1,4,32,256]{4,3,2,1,0:T(8,128)} %fields_lanes.9.refs_0_, f32[8,2,4,32,256]{4,3,2,1,0:T(8,128)} %fields_lanes.8.refs_1_, f32[8,2,4,32,256]{4,3,2,1,0:T(8,128)} %fields_lanes.7.refs_2_, f32[8,2,4,32,256]{4,3,2,1,0:T(8,128)} %fields_lanes.6.refs_3_, ...), custom_call_target="tpu_custom_call" | custom-call | flops 52428800 | bytes 37748736 | tf_op jit(solution)/shard_map/ray_step/pallas_call | solution.py:563
  (28 shorter events, 0.9 us)
Async XLA Ops:
  42.2 5.4 copy-start.2
  42.2 54.8 %all-to-all-start = ((f32[8,1,512,256]{3,2,1,0:T(8,128)}), f32[8,1,512,256]{3,2,1,0:T(8,128)}, u32[]{:S(2)}, u32[]{:S(2)}) async-start(f32[8,1,512,256]{3,2,1,0:T(8,128)} %column_lanes.5), calls=%async_computation | async-start | bytes 8388608 | tf_op jit(solution)/shard_map/all_to_all | solution.py:641
  47.5 407.9 %all-reduce.2.cloned.1.call-start = ((), (), s32[]{:S(2)}) async-start(), calls=%async_computation.15 | async-start | bytes 262144 | tf_op jit(solution)/shard_map/psum | solution.py:591
  52.5 0.5 copy-start.3
  97.0 99.4 %all-to-all-start.4 = ((f32[8,2,512,256]{3,2,1,0:T(8,128)}), f32[8,2,512,256]{3,2,1,0:T(8,128)}, u32[]{:S(2)}, u32[]{:S(2)}) async-start(f32[8,2,512,256]{3,2,1,0:T(8,128)} %column_lanes.8), calls=%async_computation.6 | async-start | bytes 16777216 | tf_op jit(solution)/shard_map/all_to_all | solution.py:641
  102.0 387.9 %reduce-scatter.8.cloned.1.call-start = ((), (), s32[]{:S(2)}) async-start(), calls=%async_computation.17 | async-start | bytes 2621440 | tf_op jit(solution)/shard_map/reduce_scatter | solution.py:659
  196.4 99.2 %all-to-all-start.1 = ((f32[8,2,512,256]{3,2,1,0:T(8,128)}), f32[8,2,512,256]{3,2,1,0:T(8,128)}, u32[]{:S(2)}, u32[]{:S(2)}) async-start(f32[8,2,512,256]{3,2,1,0:T(8,128)} %column_lanes.6), calls=%async_computation.1 | async-start | bytes 16777216 | tf_op jit(solution)/shard_map/all_to_all | solution.py:641
  201.4 302.4 %reduce-scatter.10.cloned.1.call-start = ((), (), s32[]{:S(2)}) async-start(), calls=%async_computation.18 | async-start | bytes 5242880 | tf_op jit(solution)/shard_map/reduce_scatter | solution.py:659
  295.6 99.0 %all-to-all-start.7 = ((f32[8,2,512,256]{3,2,1,0:T(8,128)}), f32[8,2,512,256]{3,2,1,0:T(8,128)}, u32[]{:S(2)}, u32[]{:S(2)}) async-start(f32[8,2,512,256]{3,2,1,0:T(8,128)} %column_lanes.9), calls=%async_computation.11 | async-start | bytes 16777216 | tf_op jit(solution)/shard_map/all_to_all | solution.py:641
  300.5 222.8 %reduce-scatter.12.cloned.1.call-start = ((), (), s32[]{:S(2)}) async-start(), calls=%async_computation.19 | async-start | bytes 5242880 | tf_op jit(solution)/shard_map/reduce_scatter | solution.py:659
  394.6 61.8 %all-to-all-start.2 = ((f32[8,1,512,256]{3,2,1,0:T(8,128)}), f32[8,1,512,256]{3,2,1,0:T(8,128)}, u32[]{:S(2)}, u32[]{:S(2)}) async-start(f32[8,1,512,256]{3,2,1,0:T(8,128)} %column_lanes.7), calls=%async_computation.2 | async-start | bytes 8388608 | tf_op jit(solution)/shard_map/all_to_all | solution.py:641
  399.2 143.1 %reduce-scatter.14.cloned.1.call-start = ((), (), s32[]{:S(2)}) async-start(), calls=%async_computation.20 | async-start | bytes 5242880 | tf_op jit(solution)/shard_map/reduce_scatter | solution.py:659
  455.3 125.1 %reduce-scatter.6.cloned.1.call-start = ((), (), s32[]{:S(2)}) async-start(), calls=%async_computation.16 | async-start | bytes 2621440 | tf_op jit(solution)/shard_map/reduce_scatter | solution.py:659
  523.4 18.9 %all-to-all-start.6 = ((f32[8,2,32,512]{3,2,1,0:T(8,128)}), f32[8,2,32,512]{3,2,1,0:T(8,128)S(1)}, u32[]{:S(2)}, u32[]{:S(2)}) async-start(f32[8,2,32,512]{3,2,1,0:T(8,128)} %bitcast.40), calls=%async_computation.10 | async-start | bytes 2097152 | tf_op jit(solution)/shard_map/all_to_all | solution.py:641
  542.3 8.5 %copy-start = (f32[8,2,32,512]{3,2,1,0:T(8,128)}, f32[8,2,32,512]{3,2,1,0:T(8,128)S(1)}, u32[]{:S(2)}) copy-start(f32[8,2,32,512]{3,2,1,0:T(8,128)S(1)} %all-to-all-done.6.t_ref) | copy-start | bytes 3145732
  542.3 21.3 %all-to-all-start.8 = ((f32[8,2,32,512]{3,2,1,0:T(8,128)}), f32[8,2,32,512]{3,2,1,0:T(8,128)}, u32[]{:S(2)}, u32[]{:S(2)}) async-start(f32[8,2,32,512]{3,2,1,0:T(8,128)} %bitcast.39), calls=%async_computation.13 | async-start | bytes 2097152 | tf_op jit(solution)/shard_map/all_to_all | solution.py:641
  580.4 13.4 %all-to-all-start.9 = ((f32[8,1,32,512]{3,2,1,0:T(8,128)}), f32[8,1,32,512]{3,2,1,0:T(8,128)S(1)}, u32[]{:S(2)}, u32[]{:S(2)}) async-start(f32[8,1,32,512]{3,2,1,0:T(8,128)} %bitcast.44), calls=%async_computation.14 | async-start | bytes 1048576 | tf_op jit(solution)/shard_map/all_to_all | solution.py:641
  593.8 0.8 copy-start.1
Sparse Core Ops, SparseCore 0:
  53.9 167.3 all-reduce.1
Sparse Core Ops, SparseCore 1:
  146.7 45.9 reduce-scatter.7
  270.1 78.8 reduce-scatter.9
  363.6 79.0 reduce-scatter.11
  455.4 78.7 reduce-scatter.13
  536.5 43.9 reduce-scatter.5
